TPU v7x, 256 devices: a whole 4x4x8 slice. The times are simulated.
256 devices in a mesh: gx: 8 (over z), gy: 8 (over x, y_lo), gz: 4 (over y_hi, core).
Axes of the slice: x: 4, y: 4 (y_hi: 2, y_lo: 2; y = y_hi * 2 + y_lo), z: 8, core: 2. Of those that a mesh axis runs over, the one named last changes fastest.
Arguments:
- data: float32 [16, 1024, 1024], P('gz', 'gx', 'gy'), may hold values from -6 to 6
- weight: float32 [16, 1024, 1024], P('gz', 'gx', 'gy'), may hold values from 0.2 to 2
- dual_start: float32 [3, 16, 1024, 1024], P(None, 'gz', 'gx', 'gy'), may hold values from -3 to 3
- dual_mid: float32 [3, 16, 1024, 1024], P(None, 'gz', 'gx', 'gy'), may hold values from -3 to 3
- cotangent: float32 [3, 16, 1024, 1024], P(None, 'gz', 'gx', 'gy'), may hold values from -6 to 6
Outputs:
- dual_grad: float32 [3, 16, 1024, 1024], P(None, 'gz', 'gx', 'gy')
- weight_grad: float32 [16, 1024, 1024], P('gz', 'gx', 'gy')
- data_grad: float32 [16, 1024, 1024], P('gz', 'gx', 'gy')
All inputs are finite; a program needn't handle non-finite values.
Results may differ from a plain program's by a relative error of at most 0.00002.
Values sent between devices are 32-bit elements; how exact they have to be, the bound alone decides.
A program may use at most 64 MiB of HBM per device.

v0:
```python
import jax
import jax.numpy as jnp
from jax import lax
from jax.sharding import PartitionSpec as P

step_size = 0.08
inverse_lambda = 0.5
smoothing = 0.01


def extended(cells, sides, width):
    for axis, dim in sides:
        count = lax.axis_size(axis)
        ends = count - 1
        head = lax.slice_in_dim(cells, 0, width, axis=dim)
        tail = lax.slice_in_dim(cells, cells.shape[dim] - width, cells.shape[dim], axis=dim)
        cells = jnp.concatenate(
            [
                lax.ppermute(tail, axis, [(i, (i + 1) % count) for i in range(ends)]),
                cells,
                lax.ppermute(head, axis, [((i + 1) % count, i) for i in range(ends)]),
            ],
            axis=dim,
        )
    return cells


def take(field, start, extent):
    return field[
        ...,
        start[0] : start[0] + extent[0],
        start[1] : start[1] + extent[1],
        start[2] : start[2] + extent[2],
    ]


def pad_cells(stack):
    slabs = extended(stack, (("gz", 1),), 1)
    return extended(slabs, (("gx", 2), ("gy", 3)), 1)


def divergence(padded, extent):
    total = None
    for axis in range(3):
        lower = [1, 1, 1]
        lower[axis] = 0
        term = take(padded[axis], (1, 1, 1), extent) - take(padded[axis], tuple(lower), extent)
        total = term if total is None else total + term
    return total


def gradient(field, base, extent):
    center = take(field, (base, base, base), extent)
    parts = []
    for axis in range(3):
        upper = [base, base, base]
        upper[axis] = base + 1
        parts.append(take(field, tuple(upper), extent) - center)
    return jnp.stack(parts)


def local_adjoint(dual, slopes, weight, cot):
    norm = jnp.sqrt(jnp.sum(slopes * slopes, axis=0) + smoothing)
    denom = 1.0 + step_size * norm / weight
    update = (dual + step_size * slopes) / denom
    inner = jnp.sum(cot * update, axis=0)
    weight_part = inner * step_size * norm / (denom * weight * weight)
    norm_scale = -inner * step_size / (denom * weight)
    slope_cot = step_size * cot / denom + norm_scale / norm * slopes
    return (slope_cot, denom, weight_part)


def shards(data, weight, dual_start, dual_mid, cotangent):
    planes, rows, cols = data.shape
    inner_ext = (planes, rows, cols)
    padded = pad_cells(jnp.concatenate([dual_start, dual_mid], 0))
    scaled = data * inverse_lambda
    values = jnp.stack(
        [divergence(padded[0:3], inner_ext) - scaled, divergence(padded[3:6], inner_ext) - scaled]
    )
    padded_values = pad_cells(values)
    slopes_start = gradient(padded_values[0], 1, inner_ext)
    slopes_mid = gradient(padded_values[1], 1, inner_ext)
    current = cotangent
    weight_parts = []
    data_parts = []
    for dual, slopes in ((dual_mid, slopes_mid), (dual_start, slopes_start)):
        slope_cot, denom, weight_part = local_adjoint(dual, slopes, weight, current)
        padded_cot = pad_cells(slope_cot)
        value_cot = -divergence(padded_cot, inner_ext)
        descent = gradient(pad_cells(value_cot[None])[0], 1, inner_ext)
        current = current / denom - descent
        weight_parts.append(weight_part)
        data_parts.append(-value_cot * inverse_lambda)
    return (current, weight_parts[1] + weight_parts[0], data_parts[1] + data_parts[0])


def solution(mesh):
    in_specs = (
        P("gz", "gx", "gy"),
        P("gz", "gx", "gy"),
        P(None, "gz", "gx", "gy"),
        P(None, "gz", "gx", "gy"),
        P(None, "gz", "gx", "gy"),
    )
    out_specs = (P(None, "gz", "gx", "gy"), P("gz", "gx", "gy"), P("gz", "gx", "gy"))
    return jax.shard_map(shards, mesh=mesh, in_specs=in_specs, out_specs=out_specs, check_vma=False)
```

profile of v0, /device:TPU:1, one launch (start us, length us, event | category | flops | bytes accessed | tf_op | source)
XLA Modules:
  0.0 273.0 jit_solution(2952771618243365797)
XLA Ops:
  2.1 6.2 %collective-permute-start = (f32[6,1,128,128]{3,2,1,0:T(8,128)S(1)}, f32[6,1,128,128]{3,2,1,0:T(8,128)S(1)}, u32[]{:S(2)}, u32[]{:S(2)}) collective-permute-start(f32[6,1,128,128]{3,2,1,0:T(8,128)S(1)} %get-tuple-element.33), channel_id=1, source_target_pairs={{0,1},{1,2},{2,3},{4,5},{5,6},{6,7},{8,9},{9,10},{10,11},{12,13},{... | collective-permute-start | bytes 1179656 | tf_op jit(solution)/shard_map/ppermute | solution.py:19
  13.0 5.9 %collective-permute-done.1 = f32[6,1,128,128]{3,2,1,0:T(8,128)S(1)} collective-permute-done((f32[6,1,128,128]{3,2,1,0:T(8,128)S(1)}, f32[6,1,128,128]{3,2,1,0:T(8,128)S(1)}, u32[]{:S(2)}, u32[]{:S(2)}) %collective-permute-start.1) | collective-permute-done | bytes 393248 | tf_op jit(solution)/shard_map/ppermute | solution.py:21
  19.0 3.5 %collective-permute-start.2 = (f32[6,6,1,128]{3,2,1,0:T(1,128)S(1)}, f32[6,6,1,128]{3,2,1,0:T(1,128)S(1)}, u32[]{:S(2)}, u32[]{:S(2)}) collective-permute-start(f32[6,6,1,128]{3,2,1,0:T(1,128)S(1)} %get-tuple-element.29), channel_id=1, source_target_pairs={{0,32},{32,64},{64,96},{96,128},{128,160},{160,192},{192,224},{1,3... | collective-permute-start | bytes 55304 | tf_op jit(solution)/shard_map/ppermute | solution.py:19
  23.8 3.4 %collective-permute-done.3 = f32[6,6,1,128]{3,2,1,0:T(1,128)S(1)} collective-permute-done((f32[6,6,1,128]{3,2,1,0:T(1,128)S(1)}, f32[6,6,1,128]{3,2,1,0:T(1,128)S(1)}, u32[]{:S(2)}, u32[]{:S(2)}) %collective-permute-start.3) | collective-permute-done | bytes 18464 | tf_op jit(solution)/shard_map/ppermute | solution.py:21
  27.5 3.1 %fusion.26 = (f32[6,6,130,1]{3,2,1,0:T(8,128)}, f32[6,6,130,1]{3,2,1,0:T(8,128)}) fusion(f32[6,6,130,128]{3,2,1,0:T(8,128)S(1)} %pad_maximum_fusion.1), kind=kLoop, calls=%fused_computation.117 | loop fusion | bytes 74880 | tf_op jit(solution)/shard_map/slice | solution.py:16
  30.5 3.1 %copy.26 = f32[6,6,130,1]{2,3,1,0:T(1,128)S(1)} copy(f32[6,6,130,1]{3,2,1,0:T(8,128)} %get-tuple-element.27) | data formatting | bytes 37440 | tf_op jit(solution)/shard_map/slice | solution.py:16
  35.9 3.1 %copy.27 = f32[6,6,130,1]{2,3,1,0:T(1,128)S(1)} copy(f32[6,6,130,1]{3,2,1,0:T(8,128)} %get-tuple-element.28) | data formatting | bytes 37440 | tf_op jit(solution)/shard_map/slice | solution.py:15
  46.5 5.5 %pad_maximum_fusion = f32[6,6,130,130]{3,2,1,0:T(8,128)S(1)} fusion(f32[6,6,130,1]{3,2,1,0:T(8,128)} %copy.29, f32[6,6,1,128]{3,2,1,0:T(1,128)S(1)} %collective-permute-done.3, f32[6,1,128,128]{3,2,1,0:T(8,128)S(1)} %collective-permute-done.1, f32[6,4,128,128]{3,2,1,0:T(8,128)S(1)} %constant_dynamic-update-slice_fusion, ...), kind=kLoop, calls=%fused_computation | loop fusion | flops 3650400 | bytes 4867200 | tf_op jit(solution)/shard_map/concatenate | solution.py:17
  53.8 4.5 %collective-permute-start.6 = (f32[2,1,128,128]{3,2,1,0:T(8,128)S(1)}, f32[2,1,128,128]{3,2,1,0:T(8,128)S(1)}, u32[]{:S(2)}, u32[]{:S(2)}) collective-permute-start(f32[2,1,128,128]{3,2,1,0:T(8,128)S(1)} %get-tuple-element.65), channel_id=1, source_target_pairs={{0,1},{1,2},{2,3},{4,5},{5,6},{6,7},{8,9},{9,10},{10,11},{12,13},{... | collective-permute-start | bytes 393224 | tf_op jit(solution)/shard_map/ppermute | solution.py:19
  60.2 5.9 %collective-permute-done.7 = f32[2,1,128,128]{3,2,1,0:T(8,128)S(1)} collective-permute-done((f32[2,1,128,128]{3,2,1,0:T(8,128)S(1)}, f32[2,1,128,128]{3,2,1,0:T(8,128)S(1)}, u32[]{:S(2)}, u32[]{:S(2)}) %collective-permute-start.7) | collective-permute-done | bytes 131104 | tf_op jit(solution)/shard_map/ppermute | solution.py:21
  66.1 3.5 %collective-permute-start.8 = (f32[2,6,1,128]{3,0,2,1:T(2,128)S(1)}, f32[2,6,1,128]{3,0,2,1:T(2,128)S(1)}, u32[]{:S(2)}, u32[]{:S(2)}) collective-permute-start(f32[2,6,1,128]{3,0,2,1:T(2,128)S(1)} %copy.30), channel_id=1, source_target_pairs={{0,32},{32,64},{64,96},{96,128},{128,160},{160,192},{192,224},{1,3... | collective-permute-start | bytes 18440 | tf_op jit(solution)/shard_map/ppermute | solution.py:19
  71.0 4.3 %collective-permute-done.9 = f32[2,6,1,128]{3,0,2,1:T(2,128)S(1)} collective-permute-done((f32[2,6,1,128]{3,0,2,1:T(2,128)S(1)}, f32[2,6,1,128]{3,0,2,1:T(2,128)S(1)}, u32[]{:S(2)}, u32[]{:S(2)}) %collective-permute-start.9) | collective-permute-done | bytes 6176 | tf_op jit(solution)/shard_map/ppermute | solution.py:21
  76.2 3.6 %collective-permute-start.10 = (f32[2,6,130,1]{2,0,3,1:T(2,128)S(1)}, f32[2,6,130,1]{2,0,3,1:T(2,128)S(1)}, u32[]{:S(2)}, u32[]{:S(2)}) collective-permute-start(f32[2,6,130,1]{2,0,3,1:T(2,128)S(1)} %copy.34), channel_id=1, source_target_pairs={{0,4},{4,8},{8,12},{12,16},{16,20},{20,24},{24,28},{1,5},{5,9},{9,... | collective-permute-start | bytes 18728 | tf_op jit(solution)/shard_map/ppermute | solution.py:19
  99.5 5.0 %collective-permute-start.12 = (f32[3,1,128,128]{3,2,1,0:T(8,128)S(1)}, f32[3,1,128,128]{3,2,1,0:T(8,128)S(1)}, u32[]{:S(2)}, u32[]{:S(2)}) collective-permute-start(f32[3,1,128,128]{3,2,1,0:T(8,128)S(1)} %get-tuple-element.61), channel_id=1, source_target_pairs={{0,1},{1,2},{2,3},{4,5},{5,6},{6,7},{8,9},{9,10},{10,11},{12,13},{... | collective-permute-start | bytes 589832 | tf_op jit(solution)/shard_map/ppermute | solution.py:19
  107.0 5.9 %collective-permute-done.13 = f32[3,1,128,128]{3,2,1,0:T(8,128)S(1)} collective-permute-done((f32[3,1,128,128]{3,2,1,0:T(8,128)S(1)}, f32[3,1,128,128]{3,2,1,0:T(8,128)S(1)}, u32[]{:S(2)}, u32[]{:S(2)}) %collective-permute-start.13) | collective-permute-done | bytes 196640 | tf_op jit(solution)/shard_map/ppermute | solution.py:21
  113.0 5.0 %collective-permute-start.14 = (f32[3,6,1,128]{3,2,1,0:T(1,128)S(1)}, f32[3,6,1,128]{3,2,1,0:T(1,128)S(1)}, u32[]{:S(2)}, u32[]{:S(2)}) collective-permute-start(f32[3,6,1,128]{3,2,1,0:T(1,128)S(1)} %get-tuple-element.41), channel_id=1, source_target_pairs={{0,32},{32,64},{64,96},{96,128},{128,160},{160,192},{192,224},{1,3... | collective-permute-start | bytes 27656 | tf_op jit(solution)/shard_map/ppermute | solution.py:19
  119.3 3.4 %collective-permute-done.15 = f32[3,6,1,128]{3,2,1,0:T(1,128)S(1)} collective-permute-done((f32[3,6,1,128]{3,2,1,0:T(1,128)S(1)}, f32[3,6,1,128]{3,2,1,0:T(1,128)S(1)}, u32[]{:S(2)}, u32[]{:S(2)}) %collective-permute-start.15) | collective-permute-done | bytes 9248 | tf_op jit(solution)/shard_map/ppermute | solution.py:21
  127.4 2.9 %collective-permute-start.16 = (f32[3,6,130,1]{2,3,1,0:T(1,128)}, f32[3,6,130,1]{2,3,1,0:T(1,128)}, u32[]{:S(2)}, u32[]{:S(2)}) collective-permute-start(f32[3,6,130,1]{2,3,1,0:T(1,128)} %copy.44), channel_id=1, source_target_pairs={{0,4},{4,8},{8,12},{12,16},{16,20},{20,24},{24,28},{1,5},{5,9},{9,... | collective-permute-start | bytes 28088 | tf_op jit(solution)/shard_map/ppermute | solution.py:19
  142.4 5.1 %collective-permute-start.18 = (f32[1,1,128,128]{3,2,1,0:T(8,128)S(1)}, f32[1,1,128,128]{3,2,1,0:T(8,128)S(1)}, u32[]{:S(2)}, u32[]{:S(2)}) collective-permute-start(f32[1,1,128,128]{3,2,1,0:T(8,128)S(1)} %get-tuple-element.77), channel_id=1, source_target_pairs={{0,1},{1,2},{2,3},{4,5},{5,6},{6,7},{8,9},{9,10},{10,11},{12,13},{... | collective-permute-start | bytes 196616 | tf_op jit(solution)/shard_map/ppermute | solution.py:19
  149.4 5.2 %collective-permute-done.19 = f32[1,1,128,128]{3,2,1,0:T(8,128)S(1)} collective-permute-done((f32[1,1,128,128]{3,2,1,0:T(8,128)S(1)}, f32[1,1,128,128]{3,2,1,0:T(8,128)S(1)}, u32[]{:S(2)}, u32[]{:S(2)}) %collective-permute-start.19) | collective-permute-done | bytes 65568 | tf_op jit(solution)/shard_map/ppermute | solution.py:21
  154.6 3.6 %collective-permute-start.20 = (f32[1,6,1,128]{3,2,1,0:T(1,128)S(1)}, f32[1,6,1,128]{3,2,1,0:T(1,128)S(1)}, u32[]{:S(2)}, u32[]{:S(2)}) collective-permute-start(f32[1,6,1,128]{3,2,1,0:T(1,128)S(1)} %get-tuple-element.73), channel_id=1, source_target_pairs={{0,32},{32,64},{64,96},{96,128},{128,160},{160,192},{192,224},{1,3... | collective-permute-start | bytes 9224 | tf_op jit(solution)/shard_map/ppermute | solution.py:19
  159.5 3.0 %collective-permute-done.21 = f32[1,6,1,128]{3,2,1,0:T(1,128)S(1)} collective-permute-done((f32[1,6,1,128]{3,2,1,0:T(1,128)S(1)}, f32[1,6,1,128]{3,2,1,0:T(1,128)S(1)}, u32[]{:S(2)}, u32[]{:S(2)}) %collective-permute-start.21) | collective-permute-done | bytes 3104 | tf_op jit(solution)/shard_map/ppermute | solution.py:21
  163.5 3.8 %collective-permute-start.22 = (f32[1,6,130,1]{3,2,1,0:T(8,128)}, f32[1,6,130,1]{3,2,1,0:T(8,128)}, u32[]{:S(2)}, u32[]{:S(2)}) collective-permute-start(f32[1,6,130,1]{3,2,1,0:T(8,128)} %get-tuple-element.69), channel_id=1, source_target_pairs={{0,4},{4,8},{8,12},{12,16},{16,20},{20,24},{24,28},{1,5},{5,9},{9,... | collective-permute-start | bytes 9368 | tf_op jit(solution)/shard_map/ppermute | solution.py:19
  168.7 14.4 %collective-permute-done.22 = f32[1,6,130,1]{3,2,1,0:T(8,128)} collective-permute-done((f32[1,6,130,1]{3,2,1,0:T(8,128)}, f32[1,6,130,1]{3,2,1,0:T(8,128)}, u32[]{:S(2)}, u32[]{:S(2)}) %collective-permute-start.22) | collective-permute-done | bytes 3152 | tf_op jit(solution)/shard_map/ppermute | solution.py:19
  195.9 5.9 %collective-permute-done.25 = f32[3,1,128,128]{3,2,1,0:T(8,128)S(1)} collective-permute-done((f32[3,1,128,128]{3,2,1,0:T(8,128)S(1)}, f32[3,1,128,128]{3,2,1,0:T(8,128)S(1)}, u32[]{:S(2)}, u32[]{:S(2)}) %collective-permute-start.25) | collective-permute-done | bytes 196640 | tf_op jit(solution)/shard_map/ppermute | solution.py:21
  206.0 3.1 %collective-permute-done.27 = f32[3,6,1,128]{3,2,1,0:T(1,128)S(1)} collective-permute-done((f32[3,6,1,128]{3,2,1,0:T(1,128)S(1)}, f32[3,6,1,128]{3,2,1,0:T(1,128)S(1)}, u32[]{:S(2)}, u32[]{:S(2)}) %collective-permute-start.27) | collective-permute-done | bytes 9248 | tf_op jit(solution)/shard_map/ppermute | solution.py:21
  213.0 3.8 %collective-permute-start.28 = (f32[3,6,130,1]{2,3,1,0:T(1,128)S(1)}, f32[3,6,130,1]{2,3,1,0:T(1,128)S(1)}, u32[]{:S(2)}, u32[]{:S(2)}) collective-permute-start(f32[3,6,130,1]{2,3,1,0:T(1,128)S(1)} %copy.54), channel_id=1, source_target_pairs={{0,4},{4,8},{8,12},{12,16},{16,20},{20,24},{24,28},{1,5},{5,9},{9,... | collective-permute-start | bytes 28088 | tf_op jit(solution)/shard_map/ppermute | solution.py:19
  230.1 5.0 %collective-permute-start.30 = (f32[1,1,128,128]{3,2,1,0:T(8,128)S(1)}, f32[1,1,128,128]{3,2,1,0:T(8,128)S(1)}, u32[]{:S(2)}, u32[]{:S(2)}) collective-permute-start(f32[1,1,128,128]{3,2,1,0:T(8,128)S(1)} %get-tuple-element.75), channel_id=1, source_target_pairs={{0,1},{1,2},{2,3},{4,5},{5,6},{6,7},{8,9},{9,10},{10,11},{12,13},{... | collective-permute-start | bytes 196616 | tf_op jit(solution)/shard_map/ppermute | solution.py:19
  237.0 5.2 %collective-permute-done.31 = f32[1,1,128,128]{3,2,1,0:T(8,128)S(1)} collective-permute-done((f32[1,1,128,128]{3,2,1,0:T(8,128)S(1)}, f32[1,1,128,128]{3,2,1,0:T(8,128)S(1)}, u32[]{:S(2)}, u32[]{:S(2)}) %collective-permute-start.31) | collective-permute-done | bytes 65568 | tf_op jit(solution)/shard_map/ppermute | solution.py:21
  246.3 3.0 %collective-permute-done.33 = f32[1,6,1,128]{3,2,1,0:T(1,128)S(1)} collective-permute-done((f32[1,6,1,128]{3,2,1,0:T(1,128)S(1)}, f32[1,6,1,128]{3,2,1,0:T(1,128)S(1)}, u32[]{:S(2)}, u32[]{:S(2)}) %collective-permute-start.33) | collective-permute-done | bytes 3104 | tf_op jit(solution)/shard_map/ppermute | solution.py:21
  249.6 3.4 %collective-permute-start.34 = (f32[1,6,130,1]{3,2,1,0:T(8,128)S(1)}, f32[1,6,130,1]{3,2,1,0:T(8,128)S(1)}, u32[]{:S(2)}, u32[]{:S(2)}) collective-permute-start(f32[1,6,130,1]{3,2,1,0:T(8,128)S(1)} %get-tuple-element.67), channel_id=1, source_target_pairs={{0,4},{4,8},{8,12},{12,16},{16,20},{20,24},{24,28},{1,5},{5,9},{9,... | collective-permute-start | bytes 9368 | tf_op jit(solution)/shard_map/ppermute | solution.py:19
  255.2 14.2 %collective-permute-done.34 = f32[1,6,130,1]{3,2,1,0:T(8,128)S(1)} collective-permute-done((f32[1,6,130,1]{3,2,1,0:T(8,128)S(1)}, f32[1,6,130,1]{3,2,1,0:T(8,128)S(1)}, u32[]{:S(2)}, u32[]{:S(2)}) %collective-permute-start.34) | collective-permute-done | bytes 3152 | tf_op jit(solution)/shard_map/ppermute | solution.py:19
  (169 shorter events, 115.0 us)
Async XLA Ops:
  2.1 10.9 %collective-permute-start = (f32[6,1,128,128]{3,2,1,0:T(8,128)S(1)}, f32[6,1,128,128]{3,2,1,0:T(8,128)S(1)}, u32[]{:S(2)}, u32[]{:S(2)}) collective-permute-start(f32[6,1,128,128]{3,2,1,0:T(8,128)S(1)} %get-tuple-element.33), channel_id=1, source_target_pairs={{0,1},{1,2},{2,3},{4,5},{5,6},{6,7},{8,9},{9,10},{10,11},{12,13},{... | collective-permute-start | bytes 1179656 | tf_op jit(solution)/shard_map/ppermute | solution.py:19
  8.3 10.6 %collective-permute-start.1 = (f32[6,1,128,128]{3,2,1,0:T(8,128)S(1)}, f32[6,1,128,128]{3,2,1,0:T(8,128)S(1)}, u32[]{:S(2)}, u32[]{:S(2)}) collective-permute-start(f32[6,1,128,128]{3,2,1,0:T(8,128)S(1)} %get-tuple-element.34), channel_id=1, source_target_pairs={{1,0},{2,1},{3,2},{5,4},{6,5},{7,6},{9,8},{10,9},{11,10},{13,12},{... | collective-permute-start | bytes 1179656 | tf_op jit(solution)/shard_map/ppermute | solution.py:21
  19.0 4.9 %collective-permute-start.2 = (f32[6,6,1,128]{3,2,1,0:T(1,128)S(1)}, f32[6,6,1,128]{3,2,1,0:T(1,128)S(1)}, u32[]{:S(2)}, u32[]{:S(2)}) collective-permute-start(f32[6,6,1,128]{3,2,1,0:T(1,128)S(1)} %get-tuple-element.29), channel_id=1, source_target_pairs={{0,32},{32,64},{64,96},{96,128},{128,160},{160,192},{192,224},{1,3... | collective-permute-start | bytes 55304 | tf_op jit(solution)/shard_map/ppermute | solution.py:19
  22.5 4.7 %collective-permute-start.3 = (f32[6,6,1,128]{3,2,1,0:T(1,128)S(1)}, f32[6,6,1,128]{3,2,1,0:T(1,128)S(1)}, u32[]{:S(2)}, u32[]{:S(2)}) collective-permute-start(f32[6,6,1,128]{3,2,1,0:T(1,128)S(1)} %get-tuple-element.30), channel_id=1, source_target_pairs={{32,0},{64,32},{96,64},{128,96},{160,128},{192,160},{224,192},{33,... | collective-permute-start | bytes 55304 | tf_op jit(solution)/shard_map/ppermute | solution.py:21
  33.6 6.7 %collective-permute-start.4 = (f32[6,6,130,1]{2,3,1,0:T(1,128)S(1)}, f32[6,6,130,1]{2,3,1,0:T(1,128)S(1)}, u32[]{:S(2)}, u32[]{:S(2)}) collective-permute-start(f32[6,6,130,1]{2,3,1,0:T(1,128)S(1)} %copy.26), channel_id=1, source_target_pairs={{0,4},{4,8},{8,12},{12,16},{16,20},{20,24},{24,28},{1,5},{5,9},{9,... | collective-permute-start | bytes 56168 | tf_op jit(solution)/shard_map/ppermute | solution.py:19
  39.0 5.2 %collective-permute-start.5 = (f32[6,6,130,1]{2,3,1,0:T(1,128)S(1)}, f32[6,6,130,1]{2,3,1,0:T(1,128)S(1)}, u32[]{:S(2)}, u32[]{:S(2)}) collective-permute-start(f32[6,6,130,1]{2,3,1,0:T(1,128)S(1)} %copy.27), channel_id=1, source_target_pairs={{4,0},{8,4},{12,8},{16,12},{20,16},{24,20},{28,24},{5,1},{9,5},{13... | collective-permute-start | bytes 56168 | tf_op jit(solution)/shard_map/ppermute | solution.py:21
  53.8 6.4 %collective-permute-start.6 = (f32[2,1,128,128]{3,2,1,0:T(8,128)S(1)}, f32[2,1,128,128]{3,2,1,0:T(8,128)S(1)}, u32[]{:S(2)}, u32[]{:S(2)}) collective-permute-start(f32[2,1,128,128]{3,2,1,0:T(8,128)S(1)} %get-tuple-element.65), channel_id=1, source_target_pairs={{0,1},{1,2},{2,3},{4,5},{5,6},{6,7},{8,9},{9,10},{10,11},{12,13},{... | collective-permute-start | bytes 393224 | tf_op jit(solution)/shard_map/ppermute | solution.py:19
  58.3 7.8 %collective-permute-start.7 = (f32[2,1,128,128]{3,2,1,0:T(8,128)S(1)}, f32[2,1,128,128]{3,2,1,0:T(8,128)S(1)}, u32[]{:S(2)}, u32[]{:S(2)}) collective-permute-start(f32[2,1,128,128]{3,2,1,0:T(8,128)S(1)} %get-tuple-element.66), channel_id=1, source_target_pairs={{1,0},{2,1},{3,2},{5,4},{6,5},{7,6},{9,8},{10,9},{11,10},{13,12},{... | collective-permute-start | bytes 393224 | tf_op jit(solution)/shard_map/ppermute | solution.py:21
  66.1 4.9 %collective-permute-start.8 = (f32[2,6,1,128]{3,0,2,1:T(2,128)S(1)}, f32[2,6,1,128]{3,0,2,1:T(2,128)S(1)}, u32[]{:S(2)}, u32[]{:S(2)}) collective-permute-start(f32[2,6,1,128]{3,0,2,1:T(2,128)S(1)} %copy.30), channel_id=1, source_target_pairs={{0,32},{32,64},{64,96},{96,128},{128,160},{160,192},{192,224},{1,3... | collective-permute-start | bytes 18440 | tf_op jit(solution)/shard_map/ppermute | solution.py:19
  69.6 5.7 %collective-permute-start.9 = (f32[2,6,1,128]{3,0,2,1:T(2,128)S(1)}, f32[2,6,1,128]{3,0,2,1:T(2,128)S(1)}, u32[]{:S(2)}, u32[]{:S(2)}) collective-permute-start(f32[2,6,1,128]{3,0,2,1:T(2,128)S(1)} %copy.31), channel_id=1, source_target_pairs={{32,0},{64,32},{96,64},{128,96},{160,128},{192,160},{224,192},{33,... | collective-permute-start | bytes 18440 | tf_op jit(solution)/shard_map/ppermute | solution.py:21
  76.2 5.5 %collective-permute-start.10 = (f32[2,6,130,1]{2,0,3,1:T(2,128)S(1)}, f32[2,6,130,1]{2,0,3,1:T(2,128)S(1)}, u32[]{:S(2)}, u32[]{:S(2)}) collective-permute-start(f32[2,6,130,1]{2,0,3,1:T(2,128)S(1)} %copy.34), channel_id=1, source_target_pairs={{0,4},{4,8},{8,12},{12,16},{16,20},{20,24},{24,28},{1,5},{5,9},{9,... | collective-permute-start | bytes 18728 | tf_op jit(solution)/shard_map/ppermute | solution.py:19
  80.2 4.4 %collective-permute-start.11 = (f32[2,6,130,1]{2,0,3,1:T(2,128)S(1)}, f32[2,6,130,1]{2,0,3,1:T(2,128)S(1)}, u32[]{:S(2)}, u32[]{:S(2)}) collective-permute-start(f32[2,6,130,1]{2,0,3,1:T(2,128)S(1)} %copy.35), channel_id=1, source_target_pairs={{4,0},{8,4},{12,8},{16,12},{20,16},{24,20},{28,24},{5,1},{9,5},{13... | collective-permute-start | bytes 18728 | tf_op jit(solution)/shard_map/ppermute | solution.py:21
  99.5 7.6 %collective-permute-start.12 = (f32[3,1,128,128]{3,2,1,0:T(8,128)S(1)}, f32[3,1,128,128]{3,2,1,0:T(8,128)S(1)}, u32[]{:S(2)}, u32[]{:S(2)}) collective-permute-start(f32[3,1,128,128]{3,2,1,0:T(8,128)S(1)} %get-tuple-element.61), channel_id=1, source_target_pairs={{0,1},{1,2},{2,3},{4,5},{5,6},{6,7},{8,9},{9,10},{10,11},{12,13},{... | collective-permute-start | bytes 589832 | tf_op jit(solution)/shard_map/ppermute | solution.py:19
  104.4 8.5 %collective-permute-start.13 = (f32[3,1,128,128]{3,2,1,0:T(8,128)S(1)}, f32[3,1,128,128]{3,2,1,0:T(8,128)S(1)}, u32[]{:S(2)}, u32[]{:S(2)}) collective-permute-start(f32[3,1,128,128]{3,2,1,0:T(8,128)S(1)} %get-tuple-element.62), channel_id=1, source_target_pairs={{1,0},{2,1},{3,2},{5,4},{6,5},{7,6},{9,8},{10,9},{11,10},{13,12},{... | collective-permute-start | bytes 589832 | tf_op jit(solution)/shard_map/ppermute | solution.py:21
  113.0 6.3 %collective-permute-start.14 = (f32[3,6,1,128]{3,2,1,0:T(1,128)S(1)}, f32[3,6,1,128]{3,2,1,0:T(1,128)S(1)}, u32[]{:S(2)}, u32[]{:S(2)}) collective-permute-start(f32[3,6,1,128]{3,2,1,0:T(1,128)S(1)} %get-tuple-element.41), channel_id=1, source_target_pairs={{0,32},{32,64},{64,96},{96,128},{128,160},{160,192},{192,224},{1,3... | collective-permute-start | bytes 27656 | tf_op jit(solution)/shard_map/ppermute | solution.py:19
  118.0 4.7 %collective-permute-start.15 = (f32[3,6,1,128]{3,2,1,0:T(1,128)S(1)}, f32[3,6,1,128]{3,2,1,0:T(1,128)S(1)}, u32[]{:S(2)}, u32[]{:S(2)}) collective-permute-start(f32[3,6,1,128]{3,2,1,0:T(1,128)S(1)} %get-tuple-element.42), channel_id=1, source_target_pairs={{32,0},{64,32},{96,64},{128,96},{160,128},{192,160},{224,192},{33,... | collective-permute-start | bytes 27656 | tf_op jit(solution)/shard_map/ppermute | solution.py:21
  127.4 5.5 %collective-permute-start.16 = (f32[3,6,130,1]{2,3,1,0:T(1,128)}, f32[3,6,130,1]{2,3,1,0:T(1,128)}, u32[]{:S(2)}, u32[]{:S(2)}) collective-permute-start(f32[3,6,130,1]{2,3,1,0:T(1,128)} %copy.44), channel_id=1, source_target_pairs={{0,4},{4,8},{8,12},{12,16},{16,20},{20,24},{24,28},{1,5},{5,9},{9,... | collective-permute-start | bytes 28088 | tf_op jit(solution)/shard_map/ppermute | solution.py:19
  131.6 4.8 %collective-permute-start.17 = (f32[3,6,130,1]{2,3,1,0:T(1,128)}, f32[3,6,130,1]{2,3,1,0:T(1,128)}, u32[]{:S(2)}, u32[]{:S(2)}) collective-permute-start(f32[3,6,130,1]{2,3,1,0:T(1,128)} %copy.45), channel_id=1, source_target_pairs={{4,0},{8,4},{12,8},{16,12},{20,16},{24,20},{28,24},{5,1},{9,5},{13... | collective-permute-start | bytes 28088 | tf_op jit(solution)/shard_map/ppermute | solution.py:21
  142.4 7.0 %collective-permute-start.18 = (f32[1,1,128,128]{3,2,1,0:T(8,128)S(1)}, f32[1,1,128,128]{3,2,1,0:T(8,128)S(1)}, u32[]{:S(2)}, u32[]{:S(2)}) collective-permute-start(f32[1,1,128,128]{3,2,1,0:T(8,128)S(1)} %get-tuple-element.77), channel_id=1, source_target_pairs={{0,1},{1,2},{2,3},{4,5},{5,6},{6,7},{8,9},{9,10},{10,11},{12,13},{... | collective-permute-start | bytes 196616 | tf_op jit(solution)/shard_map/ppermute | solution.py:19
  147.5 7.1 %collective-permute-start.19 = (f32[1,1,128,128]{3,2,1,0:T(8,128)S(1)}, f32[1,1,128,128]{3,2,1,0:T(8,128)S(1)}, u32[]{:S(2)}, u32[]{:S(2)}) collective-permute-start(f32[1,1,128,128]{3,2,1,0:T(8,128)S(1)} %get-tuple-element.78), channel_id=1, source_target_pairs={{1,0},{2,1},{3,2},{5,4},{6,5},{7,6},{9,8},{10,9},{11,10},{13,12},{... | collective-permute-start | bytes 196616 | tf_op jit(solution)/shard_map/ppermute | solution.py:21
  154.6 4.9 %collective-permute-start.20 = (f32[1,6,1,128]{3,2,1,0:T(1,128)S(1)}, f32[1,6,1,128]{3,2,1,0:T(1,128)S(1)}, u32[]{:S(2)}, u32[]{:S(2)}) collective-permute-start(f32[1,6,1,128]{3,2,1,0:T(1,128)S(1)} %get-tuple-element.73), channel_id=1, source_target_pairs={{0,32},{32,64},{64,96},{96,128},{128,160},{160,192},{192,224},{1,3... | collective-permute-start | bytes 9224 | tf_op jit(solution)/shard_map/ppermute | solution.py:19
  163.5 19.7 %collective-permute-start.22 = (f32[1,6,130,1]{3,2,1,0:T(8,128)}, f32[1,6,130,1]{3,2,1,0:T(8,128)}, u32[]{:S(2)}, u32[]{:S(2)}) collective-permute-start(f32[1,6,130,1]{3,2,1,0:T(8,128)} %get-tuple-element.69), channel_id=1, source_target_pairs={{0,4},{4,8},{8,12},{12,16},{16,20},{20,24},{24,28},{1,5},{5,9},{9,... | collective-permute-start | bytes 9368 | tf_op jit(solution)/shard_map/ppermute | solution.py:19
  167.3 15.9 %collective-permute-start.23 = (f32[1,6,130,1]{3,2,1,0:T(8,128)S(1)}, f32[1,6,130,1]{3,2,1,0:T(8,128)}, u32[]{:S(2)}, u32[]{:S(2)}) collective-permute-start(f32[1,6,130,1]{3,2,1,0:T(8,128)S(1)} %get-tuple-element.70), channel_id=1, source_target_pairs={{4,0},{8,4},{12,8},{16,12},{20,16},{24,20},{28,24},{5,1},{9,5},{13... | collective-permute-start | bytes 9368 | tf_op jit(solution)/shard_map/ppermute | solution.py:21
  191.4 4.5 %collective-permute-start.24 = (f32[3,1,128,128]{3,2,1,0:T(8,128)S(1)}, f32[3,1,128,128]{3,2,1,0:T(8,128)S(1)}, u32[]{:S(2)}, u32[]{:S(2)}) collective-permute-start(f32[3,1,128,128]{3,2,1,0:T(8,128)S(1)} %get-tuple-element.59), channel_id=1, source_target_pairs={{0,1},{1,2},{2,3},{4,5},{5,6},{6,7},{8,9},{9,10},{10,11},{12,13},{... | collective-permute-start | bytes 589832 | tf_op jit(solution)/shard_map/ppermute | solution.py:19
  193.3 8.5 %collective-permute-start.25 = (f32[3,1,128,128]{3,2,1,0:T(8,128)S(1)}, f32[3,1,128,128]{3,2,1,0:T(8,128)S(1)}, u32[]{:S(2)}, u32[]{:S(2)}) collective-permute-start(f32[3,1,128,128]{3,2,1,0:T(8,128)S(1)} %get-tuple-element.60), channel_id=1, source_target_pairs={{1,0},{2,1},{3,2},{5,4},{6,5},{7,6},{9,8},{10,9},{11,10},{13,12},{... | collective-permute-start | bytes 589832 | tf_op jit(solution)/shard_map/ppermute | solution.py:21
  204.7 4.4 %collective-permute-start.27 = (f32[3,6,1,128]{3,2,1,0:T(1,128)S(1)}, f32[3,6,1,128]{3,2,1,0:T(1,128)S(1)}, u32[]{:S(2)}, u32[]{:S(2)}) collective-permute-start(f32[3,6,1,128]{3,2,1,0:T(1,128)S(1)} %get-tuple-element.40), channel_id=1, source_target_pairs={{32,0},{64,32},{96,64},{128,96},{160,128},{192,160},{224,192},{33,... | collective-permute-start | bytes 27656 | tf_op jit(solution)/shard_map/ppermute | solution.py:21
  213.0 7.1 %collective-permute-start.28 = (f32[3,6,130,1]{2,3,1,0:T(1,128)S(1)}, f32[3,6,130,1]{2,3,1,0:T(1,128)S(1)}, u32[]{:S(2)}, u32[]{:S(2)}) collective-permute-start(f32[3,6,130,1]{2,3,1,0:T(1,128)S(1)} %copy.54), channel_id=1, source_target_pairs={{0,4},{4,8},{8,12},{12,16},{16,20},{20,24},{24,28},{1,5},{5,9},{9,... | collective-permute-start | bytes 28088 | tf_op jit(solution)/shard_map/ppermute | solution.py:19
  218.8 4.9 %collective-permute-start.29 = (f32[3,6,130,1]{2,3,1,0:T(1,128)S(1)}, f32[3,6,130,1]{2,3,1,0:T(1,128)S(1)}, u32[]{:S(2)}, u32[]{:S(2)}) collective-permute-start(f32[3,6,130,1]{2,3,1,0:T(1,128)S(1)} %copy.55), channel_id=1, source_target_pairs={{4,0},{8,4},{12,8},{16,12},{20,16},{24,20},{28,24},{5,1},{9,5},{13... | collective-permute-start | bytes 28088 | tf_op jit(solution)/shard_map/ppermute | solution.py:21
  230.1 6.9 %collective-permute-start.30 = (f32[1,1,128,128]{3,2,1,0:T(8,128)S(1)}, f32[1,1,128,128]{3,2,1,0:T(8,128)S(1)}, u32[]{:S(2)}, u32[]{:S(2)}) collective-permute-start(f32[1,1,128,128]{3,2,1,0:T(8,128)S(1)} %get-tuple-element.75), channel_id=1, source_target_pairs={{0,1},{1,2},{2,3},{4,5},{5,6},{6,7},{8,9},{9,10},{10,11},{12,13},{... | collective-permute-start | bytes 196616 | tf_op jit(solution)/shard_map/ppermute | solution.py:19
  235.1 7.1 %collective-permute-start.31 = (f32[1,1,128,128]{3,2,1,0:T(8,128)S(1)}, f32[1,1,128,128]{3,2,1,0:T(8,128)S(1)}, u32[]{:S(2)}, u32[]{:S(2)}) collective-permute-start(f32[1,1,128,128]{3,2,1,0:T(8,128)S(1)} %get-tuple-element.76), channel_id=1, source_target_pairs={{1,0},{2,1},{3,2},{5,4},{6,5},{7,6},{9,8},{10,9},{11,10},{13,12},{... | collective-permute-start | bytes 196616 | tf_op jit(solution)/shard_map/ppermute | solution.py:21
  249.6 19.8 %collective-permute-start.34 = (f32[1,6,130,1]{3,2,1,0:T(8,128)S(1)}, f32[1,6,130,1]{3,2,1,0:T(8,128)S(1)}, u32[]{:S(2)}, u32[]{:S(2)}) collective-permute-start(f32[1,6,130,1]{3,2,1,0:T(8,128)S(1)} %get-tuple-element.67), channel_id=1, source_target_pairs={{0,4},{4,8},{8,12},{12,16},{16,20},{20,24},{24,28},{1,5},{5,9},{9,... | collective-permute-start | bytes 9368 | tf_op jit(solution)/shard_map/ppermute | solution.py:19
  253.0 17.1 %collective-permute-start.35 = (f32[1,6,130,1]{3,2,1,0:T(8,128)S(1)}, f32[1,6,130,1]{3,2,1,0:T(8,128)}, u32[]{:S(2)}, u32[]{:S(2)}) collective-permute-start(f32[1,6,130,1]{3,2,1,0:T(8,128)S(1)} %get-tuple-element.68), channel_id=1, source_target_pairs={{4,0},{8,4},{12,8},{16,12},{20,16},{24,20},{28,24},{5,1},{9,5},{13... | collective-permute-start | bytes 9368 | tf_op jit(solution)/shard_map/ppermute | solution.py:21
  (27 other events, 205.5 us)
where the time goes:
time: 275 us; the launch traced here: 273 us
  starting transfers between devices  96.4 us (35%)
  waiting for transfers between devices  95 us (35%)
  local copies, waits for them, and re-layouts  48.3 us (18%)
  other arithmetic  31.7 us (12%)
    ppermute x18, starting transfers between devices, extended(): lax.ppermute(tail, axis, [(i, (i + 1) % count) for i in range(ends)])  68.9 us
    ppermute x18, waiting for transfers between devices, extended(): lax.ppermute(head, axis, [((i + 1) % count, i) for i in range(ends)])  62.8 us
    ppermute x18, waiting for transfers between devices, extended(): lax.ppermute(tail, axis, [(i, (i + 1) % count) for i in range(ends)])  32.3 us
    ppermute x18, starting transfers between devices, extended(): lax.ppermute(head, axis, [((i + 1) % count, i) for i in range(ends)])  27.5 us
    slice x16, local copies, waits for them, and re-layouts, extended(): lax.slice_in_dim(cells, cells.shape[dim] - width, cells.shape[dim], axis=...  15.9 us
    concatenate x10, other arithmetic, extended(): jnp.concatenate([lax.ppermute(tail, axis, [(i, (i + 1) % count) for i in...  12.1 us
    unnamed x53, local copies, waits for them, and re-layouts  9.19 us
    slice x5, local copies, waits for them, and re-layouts, extended(): head = lax.slice_in_dim(cells, 0, width, axis=dim)  6.78 us
  transfers between devices with their start and end apart: 36, of which 21 were waited for; matrix products, arithmetic and copies ran while one was open for 5% of the time, Pallas kernels for 0%

commit v1 on v0

v1 whole, which is shorter than its diff:
```python
import functools

import jax
import jax.numpy as jnp
from jax import lax
from jax.experimental import pallas as pl
from jax.experimental.pallas import tpu as pltpu
from jax.sharding import PartitionSpec as P

MESH = pl.DeviceIdType.MESH
TAU = 0.08
KAPPA = 0.5
DELTA = 0.01
AXES = ("gx", "gy", "gz")

NPL, NRW, NCL = 4, 128, 128
CH = 32
PAD = 8
R, Z, C = 0, 1, 2
SLOTS = (
    ((-1, 0, 0), R),
    ((1, 0, 0), R),
    ((0, -1, 0), C),
    ((0, 1, 0), C),
    ((-1, 0, 1), R),
    ((1, 0, -1), Z),
    ((0, -1, 1), C),
    ((0, 1, -1), Z),
    ((1, -1, 0), C),
    ((-1, 1, 0), R),
    ((0, 0, -1), None),
    ((0, 0, 1), None),
)
NS = len(SLOTS)
F32 = jnp.float32


def exists(pos, sizes, off):
    ok = None
    for p, n, o in zip(pos, sizes, off):
        if o == 0:
            continue
        here = p >= 1 if o < 0 else p < n - 1
        ok = here if ok is None else jnp.logical_and(ok, here)
    return ok


def kernel(
    sizes,
    data_h, weight_h, ps_h, pm_h, cot_h,
    dual_o, wg_o, dg_o,
    data, weight, cot, q_all, u, v_m, v_s, hc, gs, aux, wacc, xbuf, tbuf, tile, rcv, pln,
    in_sem, send_sem, recv_sem,
):
    pos = tuple(lax.axis_index(a) for a in AXES)
    pm, ps, cm, cs = 0, 1, 2, 3
    loads = (
        pltpu.make_async_copy(pm_h, q_all.at[pm, :, 1 : NPL + 1, PAD : PAD + NRW], in_sem.at[0]),
        pltpu.make_async_copy(data_h, data, in_sem.at[1]),
        pltpu.make_async_copy(ps_h, q_all.at[ps, :, 1 : NPL + 1, PAD : PAD + NRW], in_sem.at[2]),
        pltpu.make_async_copy(weight_h, weight, in_sem.at[3]),
        pltpu.make_async_copy(cot_h, cot, in_sem.at[4]),
    )
    for c in loads:
        c.start()

    lane = lax.broadcasted_iota(jnp.int32, (CH, NCL), 1)
    lane8 = lax.broadcasted_iota(jnp.int32, (NPL, NCL), 1)
    sub4 = lax.broadcasted_iota(jnp.int32, (NPL, NCL), 0)

    for s, (off, kind) in enumerate(SLOTS):
        @pl.when(jnp.logical_not(exists(pos, sizes, off)))
        def _():
            for e in range(4):
                if kind is None:
                    pln[e, s - 10] = jnp.zeros((NRW, NCL), F32)
                else:
                    rcv[e, s] = jnp.zeros((8, NCL), F32)

    barrier = pltpu.get_barrier_semaphore()
    for off, _ in SLOTS:
        @pl.when(exists(pos, sizes, off))
        def _():
            peer = tuple(p + o for p, o in zip(pos, off))
            pl.semaphore_signal(barrier, inc=1, device_id=peer, device_id_type=MESH)

    for e in range(4):
        q_all[e, 0, 0, PAD : PAD + NRW] = jnp.zeros((NRW, NCL), F32)
        for k in range(NPL):
            q_all[e, 1, k + 1, 0:PAD] = jnp.zeros((PAD, NCL), F32)

    peers = sum(jnp.where(exists(pos, sizes, off), 1, 0) for off, _ in SLOTS)
    pl.semaphore_wait(barrier, peers)

    def message(e, s):
        off, kind = SLOTS[s]
        if kind is None:
            src = q_all.at[e, 0, NPL, PAD : PAD + NRW] if s == 10 else u.at[e, 0]
            dst = pln.at[e, s - 10]
        else:
            src = tile.at[e, 8 * kind : 8 * kind + 8]
            dst = rcv.at[e, s]
        peer = tuple(p - o for p, o in zip(pos, off))
        return pltpu.make_async_remote_copy(
            src_ref=src, dst_ref=dst, send_sem=send_sem.at[e, s], recv_sem=recv_sem.at[e, s],
            device_id=peer, device_id_type=MESH,
        )

    def send(e, s):
        off = SLOTS[s][0]
        @pl.when(exists(pos, sizes, tuple(-o for o in off)))
        def _():
            message(e, s).start()

    def arrive(e, s):
        @pl.when(exists(pos, sizes, SLOTS[s][0]))
        def _():
            message(e, s).wait_recv()

    def divide_part(e, k, j, extra):
        rows = slice(PAD + CH * j, PAD + CH * (j + 1))
        above = slice(PAD + CH * j - 1, PAD + CH * (j + 1) - 1)
        out = slice(CH * j, CH * (j + 1))
        q2 = q_all[e, 2, k + 1, rows]
        total = q_all[e, 0, k + 1, rows] - q_all[e, 0, k, rows]
        total = total + (q_all[e, 1, k + 1, rows] - q_all[e, 1, k + 1, above])
        total = total + (q2 - jnp.where(lane == 0, 0.0, pltpu.roll(q2, 1, 1)))
        if extra:
            total = total - KAPPA * data[k, out]
        u[e, k, out] = total
        x = jnp.where(lane == k, pltpu.roll(q2, k + 1, 1), xbuf[out])
        xbuf[out] = jnp.where(lane == k + NPL, pltpu.roll(total, k + NPL, 1), x)

    def send_all(e):
        for j in range(NRW // CH):
            rows = slice(PAD + CH * j, PAD + CH * (j + 1))
            out = slice(CH * j, CH * (j + 1))
            xbuf[out] = jnp.where(lane == 8, pltpu.roll(q_all[e, 0, NPL, rows], 8, 1), xbuf[out])
        send(e, 10)
        send(e, 11)
        xt = jnp.transpose(xbuf[...])
        tile[e, 16:24] = xt[0:8]
        tile[e, 9:10] = xt[8:9]
        tile[e, 8:9] = q_all[e, 0, NPL, PAD : PAD + 1]
        for k in range(NPL):
            tile[e, k : k + 1] = q_all[e, 1, k + 1, PAD + NRW - 1 : PAD + NRW]
            tile[e, k + NPL : k + NPL + 1] = u[e, k, 0:1]
        for s in range(10):
            send(e, s)

    def receive(e, v):
        for s in range(NS):
            arrive(e, s)
        up_x = exists(pos, sizes, (1, 0, 0))
        up_y = exists(pos, sizes, (0, 1, 0))
        up_z = exists(pos, sizes, (0, 0, 1))
        low_c = rcv[e, 2, 0:NPL]
        high_c = rcv[e, 3, NPL : 2 * NPL] - tile[e, 16 : 16 + NPL]
        high_c = high_c - jnp.where(sub4 == 0, rcv[e, 7, 1:2], 0.0)
        high_c = high_c - jnp.where(lane8 == 0, rcv[e, 9, 0:NPL], 0.0)
        high_c = jnp.where(up_y, high_c, 0.0)
        tbuf[0:NPL] = low_c
        tbuf[NPL : 2 * NPL] = high_c
        tbuf[8:16] = rcv[e, 6]
        tbuf[...] = jnp.transpose(tbuf[...])

        def planes(k, _):
            for j in range(NRW // CH):
                out = slice(CH * j, CH * (j + 1))
                col = pltpu.roll(tbuf[out], NCL - k, 1)
                v[k, out] = u[e, k, out] - jnp.where(lane == 0, col, 0.0)
            return 0

        lax.fori_loop(0, NPL, planes, 0)
        high_r = rcv[e, 1, NPL : 2 * NPL] - tile[e, 0:NPL]
        high_r = high_r - jnp.where(sub4 == 0, rcv[e, 5, 0:1], 0.0)
        high_r = high_r - jnp.where(lane8 == 0, rcv[e, 8, 0:NPL], 0.0)
        high_r = jnp.where(up_x, high_r, 0.0)
        for k in range(NPL):
            v[k, 0:1] = v[k, 0:1] - rcv[e, 0, k : k + 1]
            v[k, NRW : NRW + 1] = high_r[k : k + 1]
        for j in range(NRW // CH):
            rows = slice(PAD + CH * j, PAD + CH * (j + 1))
            out = slice(CH * j, CH * (j + 1))
            v[0, out] = v[0, out] - pln[e, 0, out]
            col = jnp.where(lane == 0, pltpu.roll(tbuf[out], NCL - 8, 1), 0.0)
            v[NPL, out] = jnp.where(up_z, pln[e, 1, out] - q_all[e, 0, NPL, rows] - col, 0.0)
        v[NPL, 0:1] = v[NPL, 0:1] - jnp.where(up_z, rcv[e, 4, 0:1], 0.0)

    def slopes(v, k, j):
        out = slice(CH * j, CH * (j + 1))
        c = v[k, out]
        col = pltpu.roll(tbuf[out], NCL - 1 - NPL - k, 1)
        return (
            v[k + 1, out] - c,
            v[k, CH * j + 1 : CH * (j + 1) + 1] - c,
            jnp.where(lane == NCL - 1, col, pltpu.roll(c, NCL - 1, 1)) - c,
        )

    def each_chunk(body):
        def planes(k, _):
            for j in range(NRW // CH):
                body(k, j)
            return 0
        lax.fori_loop(0, NPL, planes, 0)

    def spots(j):
        return slice(PAD + CH * j, PAD + CH * (j + 1)), slice(CH * j, CH * (j + 1))

    loads[0].wait()
    loads[1].wait()
    each_chunk(lambda k, j: divide_part(pm, k, j, True))
    send_all(pm)
    loads[2].wait()
    each_chunk(lambda k, j: divide_part(ps, k, j, True))
    send_all(ps)
    loads[3].wait()
    loads[4].wait()

    receive(pm, v_m)

    def adjoint_mid(k, j):
        rows, out = spots(j)
        g = slopes(v_m, k, j)
        t = g[0] * g[0] + g[1] * g[1] + g[2] * g[2] + DELTA
        rn = lax.rsqrt(t)
        n = t * rn
        w = weight[k, out]
        r = 1.0 / (w + TAU * n)
        h = w * r
        c = [cot[a, k, out] for a in range(3)]
        s = None
        for a in range(3):
            term = c[a] * (q_all[pm, a, k + 1, rows] + TAU * g[a])
            s = term if s is None else s + term
        m = TAU * r * (h * s)
        wacc[k, out] = m * n
        f = m * rn
        for a in range(3):
            hc_a = h * c[a]
            hc[a, k, out] = hc_a
            q_all[cm, a, k + 1, rows] = TAU * hc_a - f * g[a]
        divide_part(cm, k, j, False)

    each_chunk(adjoint_mid)
    send_all(cm)

    receive(ps, v_s)

    def prepare_start(k, j):
        rows, out = spots(j)
        g = slopes(v_s, k, j)
        t = g[0] * g[0] + g[1] * g[1] + g[2] * g[2] + DELTA
        rn = lax.rsqrt(t)
        n = t * rn
        w = weight[k, out]
        r = 1.0 / (w + TAU * n)
        h = w * r
        a1 = TAU * r * h
        aux[0, k, out] = h
        aux[1, k, out] = a1 * rn
        aux[2, k, out] = a1 * n
        for a in range(3):
            gs[a, k, out] = g[a]

    each_chunk(prepare_start)

    receive(cm, v_m)

    def adjoint_start(k, j):
        rows, out = spots(j)
        d = slopes(v_m, k, j)
        h = aux[0, k, out]
        g = [gs[a, k, out] for a in range(3)]
        c = [hc[a, k, out] + d[a] for a in range(3)]
        s = None
        for a in range(3):
            term = c[a] * (q_all[ps, a, k + 1, rows] + TAU * g[a])
            s = term if s is None else s + term
        wacc[k, out] = wacc[k, out] + aux[2, k, out] * s
        f = aux[1, k, out] * s
        for a in range(3):
            hc_a = h * c[a]
            hc[a, k, out] = hc_a
            q_all[cs, a, k + 1, rows] = TAU * hc_a - f * g[a]
        divide_part(cs, k, j, False)

    each_chunk(adjoint_start)
    send_all(cs)

    def finish_weight(k, j):
        _, out = spots(j)
        wg_o[k, out] = wacc[k, out] / weight[k, out]

    each_chunk(finish_weight)
    receive(cs, v_s)

    def finish(k, j):
        _, out = spots(j)
        d = slopes(v_s, k, j)
        for a in range(3):
            dual_o[a, k, out] = hc[a, k, out] + d[a]
        dg_o[k, out] = KAPPA * (v_s[k, out] + v_m[k, out])

    each_chunk(finish)
    for e in range(4):
        for s in range(NS):
            off = SLOTS[s][0]
            @pl.when(exists(pos, sizes, tuple(-o for o in off)))
            def _():
                message(e, s).wait_send()


def shards(sizes, data, weight, dual_start, dual_mid, cotangent):
    field = (NPL, NRW, NCL)
    vm = pltpu.VMEM
    whole = pl.BlockSpec(memory_space=pltpu.VMEM)
    return pl.pallas_call(
        functools.partial(kernel, sizes),
        out_shape=(
            jax.ShapeDtypeStruct((3,) + field, F32),
            jax.ShapeDtypeStruct(field, F32),
            jax.ShapeDtypeStruct(field, F32),
        ),
        in_specs=[pl.BlockSpec(memory_space=pl.ANY)] * 5,
        out_specs=(whole,) * 3,
        scratch_shapes=[
            vm(field, F32),
            vm(field, F32),
            vm((3,) + field, F32),
            vm((4, 3, NPL + 1, NRW + PAD, NCL), F32),
            vm((4,) + field, F32),
            vm((NPL + 1, NRW + PAD, NCL), F32),
            vm((NPL + 1, NRW + PAD, NCL), F32),
            vm((3,) + field, F32),
            vm((3,) + field, F32),
            vm((3,) + field, F32),
            vm(field, F32),
            vm((NRW, NCL), F32),
            vm((NRW, NCL), F32),
            vm((4, 24, NCL), F32),
            vm((4, 10, 8, NCL), F32),
            vm((4, 2, NRW, NCL), F32),
            pltpu.SemaphoreType.DMA((5,)),
            pltpu.SemaphoreType.DMA((4, NS)),
            pltpu.SemaphoreType.DMA((4, NS)),
        ],
        compiler_params=pltpu.CompilerParams(
            collective_id=0, has_side_effects=True, vmem_limit_bytes=40 * 1024 * 1024
        ),
    )(data, weight, dual_start, dual_mid, cotangent)


def solution(mesh):
    field, triple = P("gz", "gx", "gy"), P(None, "gz", "gx", "gy")
    sizes = tuple(mesh.shape[a] for a in AXES)
    return jax.shard_map(
        functools.partial(shards, sizes),
        mesh=mesh,
        in_specs=(field, field, triple, triple, triple),
        out_specs=(triple, field, field),
        check_vma=False,
    )
```

time: 275 us -> 33.1 us (0.12)
  the two profiles are of different devices: /device:TPU:1 before, /device:TPU:103 now
where the time goes in v1:
time: 33.1 us; the launch traced here: 32.8 us
  Pallas kernels  24.6 us (74%)
  local copies, waits for them, and re-layouts  7.58 us (23%)
  between operations  0.65 us (2%)
    pallas_call x1, Pallas kernels, shards(): pl.pallas_call(functools.partial(kernel, sizes), out_shape=(jax.ShapeDtyp...  24.6 us
    unnamed x13, local copies, waits for them, and re-layouts  7.58 us

profile of v1, /device:TPU:103, one launch (start us, length us, event | category | flops | bytes accessed | tf_op | source)
XLA Modules:
  0.0 32.8 jit_solution(8452778468724022888)
XLA Ops:
  0.6 0.0 copy-start
  0.6 1.1 %copy-done = f32[3,4,128,128]{3,2,1,0:T(8,128)S(1)} copy-done((f32[3,4,128,128]{3,2,1,0:T(8,128)S(1)}, f32[3,4,128,128]{3,2,1,0:T(8,128)}, u32[]{:S(2)}) %copy-start) | copy-done | bytes 786456
  1.8 0.0 copy-start.1
  1.8 1.1 %copy-done.1 = f32[3,4,128,128]{3,2,1,0:T(8,128)S(1)} copy-done((f32[3,4,128,128]{3,2,1,0:T(8,128)S(1)}, f32[3,4,128,128]{3,2,1,0:T(8,128)}, u32[]{:S(2)}) %copy-start.1) | copy-done | bytes 786456
  2.9 0.0 copy-start.2
  2.9 1.1 %copy-done.2 = f32[3,4,128,128]{3,2,1,0:T(8,128)S(1)} copy-done((f32[3,4,128,128]{3,2,1,0:T(8,128)S(1)}, f32[3,4,128,128]{3,2,1,0:T(8,128)}, u32[]{:S(2)}) %copy-start.2) | copy-done | bytes 786456
  4.0 0.0 copy-start.3
  4.0 0.9 %copy-done.3 = f32[4,128,128]{2,1,0:T(8,128)S(1)} copy-done((f32[4,128,128]{2,1,0:T(8,128)S(1)}, f32[4,128,128]{2,1,0:T(8,128)}, u32[]{:S(2)}) %copy-start.3) | copy-done | bytes 262168
  5.0 0.0 copy-start.4
  5.0 0.9 %copy-done.4 = f32[4,128,128]{2,1,0:T(8,128)S(1)} copy-done((f32[4,128,128]{2,1,0:T(8,128)S(1)}, f32[4,128,128]{2,1,0:T(8,128)}, u32[]{:S(2)}) %copy-start.4) | copy-done | bytes 262168
  5.9 24.6 %shard_map.76 = (f32[3,4,128,128]{3,2,1,0:T(8,128)S(1)}, f32[4,128,128]{2,1,0:T(8,128)S(1)}, f32[4,128,128]{2,1,0:T(8,128)S(1)}) custom-call(f32[4,128,128]{2,1,0:T(8,128)S(1)} %copy-done.3, f32[4,128,128]{2,1,0:T(8,128)S(1)} %copy-done.4, f32[3,4,128,128]{3,2,1,0:T(8,128)S(1)} %copy-done, f32[3,4,128,128]{3,2,1,0:T(8,128)S(1)} %copy-done.1, ...), custom_call_target="tpu_custom_call" | custom-call | tf_op jit(solution)/shard_map/pallas_call | solution.py:318
  30.6 0.9 %copy.11 = f32[3,4,128,128]{3,2,1,0:T(8,128)} copy(f32[3,4,128,128]{3,2,1,0:T(8,128)S(1)} %get-tuple-element.6) | data formatting | bytes 1572864
  31.4 0.7 %copy.12 = f32[4,128,128]{2,1,0:T(8,128)} copy(f32[4,128,128]{2,1,0:T(8,128)S(1)} %get-tuple-element.7) | data formatting | bytes 524288
  32.1 0.7 %copy.13 = f32[4,128,128]{2,1,0:T(8,128)} copy(f32[4,128,128]{2,1,0:T(8,128)S(1)} %get-tuple-element.8) | data formatting | bytes 524288
Async XLA Ops:
  0.6 1.1 %copy-start = (f32[3,4,128,128]{3,2,1,0:T(8,128)S(1)}, f32[3,4,128,128]{3,2,1,0:T(8,128)}, u32[]{:S(2)}) copy-start(f32[3,4,128,128]{3,2,1,0:T(8,128)} %ps_h.1) | copy-start | bytes 2359300
  1.8 1.1 %copy-start.1 = (f32[3,4,128,128]{3,2,1,0:T(8,128)S(1)}, f32[3,4,128,128]{3,2,1,0:T(8,128)}, u32[]{:S(2)}) copy-start(f32[3,4,128,128]{3,2,1,0:T(8,128)} %pm_h.1) | copy-start | bytes 2359300
  2.9 1.1 %copy-start.2 = (f32[3,4,128,128]{3,2,1,0:T(8,128)S(1)}, f32[3,4,128,128]{3,2,1,0:T(8,128)}, u32[]{:S(2)}) copy-start(f32[3,4,128,128]{3,2,1,0:T(8,128)} %cot_h.1) | copy-start | bytes 2359300
  4.0 0.9 %copy-start.3 = (f32[4,128,128]{2,1,0:T(8,128)S(1)}, f32[4,128,128]{2,1,0:T(8,128)}, u32[]{:S(2)}) copy-start(f32[4,128,128]{2,1,0:T(8,128)} %data_h.1) | copy-start | bytes 786436
  5.0 0.9 %copy-start.4 = (f32[4,128,128]{2,1,0:T(8,128)S(1)}, f32[4,128,128]{2,1,0:T(8,128)}, u32[]{:S(2)}) copy-start(f32[4,128,128]{2,1,0:T(8,128)} %weight_h.1) | copy-start | bytes 786436

commit v2 on v1

--- a/solution.py
+++ b/solution.py
@@ -35,21 +35,11 @@
 F32 = jnp.float32
 
 
-def exists(pos, sizes, off):
-    ok = None
-    for p, n, o in zip(pos, sizes, off):
-        if o == 0:
-            continue
-        here = p >= 1 if o < 0 else p < n - 1
-        ok = here if ok is None else jnp.logical_and(ok, here)
-    return ok
-
-
 def kernel(
     sizes,
     data_h, weight_h, ps_h, pm_h, cot_h,
     dual_o, wg_o, dg_o,
-    data, weight, cot, q_all, u, v_m, v_s, hc, gs, aux, wacc, xbuf, tbuf, tile, rcv, pln,
+    data, weight, cot, q_all, u, v_m, v_s, hc, gs, aux, wacc, xbuf, tbuf, tile, rcv, pln, spare,
     in_sem, send_sem, recv_sem,
 ):
     pos = tuple(lax.axis_index(a) for a in AXES)
@@ -68,54 +58,58 @@
     lane8 = lax.broadcasted_iota(jnp.int32, (NPL, NCL), 1)
     sub4 = lax.broadcasted_iota(jnp.int32, (NPL, NCL), 0)
 
-    for s, (off, kind) in enumerate(SLOTS):
-        @pl.when(jnp.logical_not(exists(pos, sizes, off)))
-        def _():
-            for e in range(4):
-                if kind is None:
-                    pln[e, s - 10] = jnp.zeros((NRW, NCL), F32)
-                else:
-                    rcv[e, s] = jnp.zeros((8, NCL), F32)
-
+    low_x, low_y, low_z = (p > 0 for p in pos)
+    up_x, up_y, up_z = (p < n - 1 for p, n in zip(pos, sizes))
+
+    def exists(off):
+        ok = None
+        for o, low, up in zip(off, (low_x, low_y, low_z), (up_x, up_y, up_z)):
+            if o != 0:
+                here = low if o < 0 else up
+                ok = here if ok is None else jnp.logical_and(ok, here)
+        return ok
+
+    has = [exists(off) for off, _ in SLOTS]
+    takes = [exists(tuple(-o for o in off)) for off, _ in SLOTS]
     barrier = pltpu.get_barrier_semaphore()
-    for off, _ in SLOTS:
-        @pl.when(exists(pos, sizes, off))
+    for (off, _), here in zip(SLOTS, has):
+        @pl.when(here)
         def _():
             peer = tuple(p + o for p, o in zip(pos, off))
             pl.semaphore_signal(barrier, inc=1, device_id=peer, device_id_type=MESH)
+
+    for side, here in ((0, low_z), (1, up_z)):
+        @pl.when(jnp.logical_not(here))
+        def _():
+            for e in range(4):
+                pln[e, side] = jnp.zeros((NRW, NCL), F32)
 
     for e in range(4):
         q_all[e, 0, 0, PAD : PAD + NRW] = jnp.zeros((NRW, NCL), F32)
         for k in range(NPL):
             q_all[e, 1, k + 1, 0:PAD] = jnp.zeros((PAD, NCL), F32)
 
-    peers = sum(jnp.where(exists(pos, sizes, off), 1, 0) for off, _ in SLOTS)
-    pl.semaphore_wait(barrier, peers)
+    pl.semaphore_wait(barrier, sum(jnp.where(here, 1, 0) for here in has))
 
     def message(e, s):
         off, kind = SLOTS[s]
         if kind is None:
             src = q_all.at[e, 0, NPL, PAD : PAD + NRW] if s == 10 else u.at[e, 0]
-            dst = pln.at[e, s - 10]
+            dst, sem = pln.at[e, s - 10], s - 9
         else:
-            src = tile.at[e, 8 * kind : 8 * kind + 8]
-            dst = rcv.at[e, s]
-        peer = tuple(p - o for p, o in zip(pos, off))
+            src, dst, sem = tile.at[e, 8 * kind : 8 * kind + 8], rcv.at[e, s], 0
         return pltpu.make_async_remote_copy(
-            src_ref=src, dst_ref=dst, send_sem=send_sem.at[e, s], recv_sem=recv_sem.at[e, s],
-            device_id=peer, device_id_type=MESH,
+            src_ref=src, dst_ref=dst, send_sem=send_sem.at[e, sem], recv_sem=recv_sem.at[e, sem],
+            device_id=tuple(p - o for p, o in zip(pos, off)), device_id_type=MESH,
         )
 
-    def send(e, s):
-        off = SLOTS[s][0]
-        @pl.when(exists(pos, sizes, tuple(-o for o in off)))
-        def _():
-            message(e, s).start()
-
-    def arrive(e, s):
-        @pl.when(exists(pos, sizes, SLOTS[s][0]))
-        def _():
-            message(e, s).wait_recv()
+    def filler(e, s, sem):
+        kind = SLOTS[s][1]
+        dst = rcv.at[e, s] if sem is recv_sem else spare.at[e, s]
+        return pltpu.make_async_copy(tile.at[e, 8 * kind : 8 * kind + 8], dst, sem.at[e, 0])
+
+    def tiles_done(e, sem):
+        pltpu.make_async_copy(rcv.at[e], rcv.at[e], sem.at[e, 0]).wait()
 
     def divide_part(e, k, j, extra):
         rows = slice(PAD + CH * j, PAD + CH * (j + 1))
@@ -136,8 +130,8 @@
             rows = slice(PAD + CH * j, PAD + CH * (j + 1))
             out = slice(CH * j, CH * (j + 1))
             xbuf[out] = jnp.where(lane == 8, pltpu.roll(q_all[e, 0, NPL, rows], 8, 1), xbuf[out])
-        send(e, 10)
-        send(e, 11)
+        pl.when(up_z)(lambda: message(e, 10).start())
+        pl.when(low_z)(lambda: message(e, 11).start())
         xt = jnp.transpose(xbuf[...])
         tile[e, 16:24] = xt[0:8]
         tile[e, 9:10] = xt[8:9]
@@ -146,22 +140,20 @@
             tile[e, k : k + 1] = q_all[e, 1, k + 1, PAD + NRW - 1 : PAD + NRW]
             tile[e, k + NPL : k + NPL + 1] = u[e, k, 0:1]
         for s in range(10):
-            send(e, s)
+            pl.when(takes[s])(lambda: message(e, s).start())
+            pl.when(jnp.logical_not(takes[s]))(lambda: filler(e, s, send_sem).start())
+            pl.when(jnp.logical_not(has[s]))(lambda: filler(e, s, recv_sem).start())
 
     def receive(e, v):
-        for s in range(NS):
-            arrive(e, s)
-        up_x = exists(pos, sizes, (1, 0, 0))
-        up_y = exists(pos, sizes, (0, 1, 0))
-        up_z = exists(pos, sizes, (0, 0, 1))
-        low_c = rcv[e, 2, 0:NPL]
+        tiles_done(e, recv_sem)
+        low_c = jnp.where(low_y, rcv[e, 2, 0:NPL], 0.0)
         high_c = rcv[e, 3, NPL : 2 * NPL] - tile[e, 16 : 16 + NPL]
-        high_c = high_c - jnp.where(sub4 == 0, rcv[e, 7, 1:2], 0.0)
-        high_c = high_c - jnp.where(lane8 == 0, rcv[e, 9, 0:NPL], 0.0)
+        high_c = high_c - jnp.where(jnp.logical_and(sub4 == 0, low_z), rcv[e, 7, 1:2], 0.0)
+        high_c = high_c - jnp.where(jnp.logical_and(lane8 == 0, low_x), rcv[e, 9, 0:NPL], 0.0)
         high_c = jnp.where(up_y, high_c, 0.0)
         tbuf[0:NPL] = low_c
         tbuf[NPL : 2 * NPL] = high_c
-        tbuf[8:16] = rcv[e, 6]
+        tbuf[8:16] = jnp.where(low_y, rcv[e, 6], 0.0)
         tbuf[...] = jnp.transpose(tbuf[...])
 
         def planes(k, _):
@@ -173,19 +165,22 @@
 
         lax.fori_loop(0, NPL, planes, 0)
         high_r = rcv[e, 1, NPL : 2 * NPL] - tile[e, 0:NPL]
-        high_r = high_r - jnp.where(sub4 == 0, rcv[e, 5, 0:1], 0.0)
-        high_r = high_r - jnp.where(lane8 == 0, rcv[e, 8, 0:NPL], 0.0)
+        high_r = high_r - jnp.where(jnp.logical_and(sub4 == 0, low_z), rcv[e, 5, 0:1], 0.0)
+        high_r = high_r - jnp.where(jnp.logical_and(lane8 == 0, low_y), rcv[e, 8, 0:NPL], 0.0)
         high_r = jnp.where(up_x, high_r, 0.0)
+        low_r = jnp.where(low_x, rcv[e, 0, 0:NPL], 0.0)
         for k in range(NPL):
-            v[k, 0:1] = v[k, 0:1] - rcv[e, 0, k : k + 1]
+            v[k, 0:1] = v[k, 0:1] - low_r[k : k + 1]
             v[k, NRW : NRW + 1] = high_r[k : k + 1]
+        pl.when(low_z)(lambda: message(e, 10).wait_recv())
+        pl.when(up_z)(lambda: message(e, 11).wait_recv())
         for j in range(NRW // CH):
             rows = slice(PAD + CH * j, PAD + CH * (j + 1))
             out = slice(CH * j, CH * (j + 1))
             v[0, out] = v[0, out] - pln[e, 0, out]
             col = jnp.where(lane == 0, pltpu.roll(tbuf[out], NCL - 8, 1), 0.0)
             v[NPL, out] = jnp.where(up_z, pln[e, 1, out] - q_all[e, 0, NPL, rows] - col, 0.0)
-        v[NPL, 0:1] = v[NPL, 0:1] - jnp.where(up_z, rcv[e, 4, 0:1], 0.0)
+        v[NPL, 0:1] = v[NPL, 0:1] - jnp.where(jnp.logical_and(up_z, low_x), rcv[e, 4, 0:1], 0.0)
 
     def slopes(v, k, j):
         out = slice(CH * j, CH * (j + 1))
@@ -304,24 +299,33 @@
 
     each_chunk(finish)
     for e in range(4):
-        for s in range(NS):
-            off = SLOTS[s][0]
-            @pl.when(exists(pos, sizes, tuple(-o for o in off)))
-            def _():
-                message(e, s).wait_send()
+        tiles_done(e, send_sem)
+        pl.when(up_z)(lambda: message(e, 10).wait_send())
+        pl.when(low_z)(lambda: message(e, 11).wait_send())
+
+
+def write_out(*refs):
+    sem = refs[-1]
+    copies = [pltpu.make_async_copy(refs[i], refs[i + 3], sem.at[i]) for i in range(3)]
+    for c in copies:
+        c.start()
+    for c in copies:
+        c.wait()
 
 
 def shards(sizes, data, weight, dual_start, dual_mid, cotangent):
     field = (NPL, NRW, NCL)
     vm = pltpu.VMEM
     whole = pl.BlockSpec(memory_space=pltpu.VMEM)
-    return pl.pallas_call(
+    shapes = (
+        jax.ShapeDtypeStruct((3,) + field, F32),
+        jax.ShapeDtypeStruct(field, F32),
+        jax.ShapeDtypeStruct(field, F32),
+    )
+    args = (data, weight, dual_start, dual_mid, cotangent)
+    results = pl.pallas_call(
         functools.partial(kernel, sizes),
-        out_shape=(
-            jax.ShapeDtypeStruct((3,) + field, F32),
-            jax.ShapeDtypeStruct(field, F32),
-            jax.ShapeDtypeStruct(field, F32),
-        ),
+        out_shape=shapes,
         in_specs=[pl.BlockSpec(memory_space=pl.ANY)] * 5,
         out_specs=(whole,) * 3,
         scratch_shapes=[
@@ -341,14 +345,22 @@
             vm((4, 24, NCL), F32),
             vm((4, 10, 8, NCL), F32),
             vm((4, 2, NRW, NCL), F32),
+            vm((4, 10, 8, NCL), F32),
             pltpu.SemaphoreType.DMA((5,)),
-            pltpu.SemaphoreType.DMA((4, NS)),
-            pltpu.SemaphoreType.DMA((4, NS)),
+            pltpu.SemaphoreType.DMA((4, 3)),
+            pltpu.SemaphoreType.DMA((4, 3)),
         ],
         compiler_params=pltpu.CompilerParams(
             collective_id=0, has_side_effects=True, vmem_limit_bytes=40 * 1024 * 1024
         ),
-    )(data, weight, dual_start, dual_mid, cotangent)
+    )(*[pltpu.with_memory_space_constraint(x, pltpu.HBM) for x in args])
+    return pl.pallas_call(
+        write_out,
+        out_shape=shapes,
+        in_specs=[pl.BlockSpec(memory_space=pltpu.VMEM)] * 3,
+        out_specs=(pl.BlockSpec(memory_space=pl.ANY),) * 3,
+        scratch_shapes=[pltpu.SemaphoreType.DMA((3,))],
+    )(*[pltpu.with_memory_space_constraint(x, pltpu.VMEM) for x in results])
 
 
 def solution(mesh):

time: 33.1 us -> 25.3 us (0.76)
  local copies, waits for them, and re-layouts: 7.58 us -> 0 us
    unnamed x13 -> x0, local copies, waits for them, and re-layouts: 7.58 us -> none
    pallas_call x1 -> x2, Pallas kernels: 24.6 us -> 24.5 us  [the longest x1 23.5 us: shards(): pl.pallas_call(functools.partial(kernel, sizes), out_shape=shapes, in_spe...]
where the time goes in v2:
time: 25.3 us; the launch traced here: 25.2 us
  Pallas kernels  24.5 us (97%)
  between operations  0.64 us (3%)
    pallas_call x1, Pallas kernels, shards(): pl.pallas_call(functools.partial(kernel, sizes), out_shape=shapes, in_spe...  23.5 us
    pallas_call x1, Pallas kernels, shards(): pl.pallas_call(write_out, out_shape=shapes, in_specs=[pl.BlockSpec(memory...  1.08 us

profile of v2, /device:TPU:103, one launch (start us, length us, event | category | flops | bytes accessed | tf_op | source)
XLA Modules:
  0.0 25.2 jit_solution(6874283026386585957)
XLA Ops:
  0.6 23.5 %shard_map.76 = (f32[3,4,128,128]{3,2,1,0:T(8,128)S(1)}, f32[4,128,128]{2,1,0:T(8,128)S(1)}, f32[4,128,128]{2,1,0:T(8,128)S(1)}) custom-call(f32[4,128,128]{2,1,0:T(8,128)} %data_h.1, f32[4,128,128]{2,1,0:T(8,128)} %weight_h.1, f32[3,4,128,128]{3,2,1,0:T(8,128)} %ps_h.1, f32[3,4,128,128]{3,2,1,0:T(8,128)} %pm_h.1, f32[3,4,128,128]{3,2,1,0:T(8,128)} %cot_h.1), custom_call_target="tpu_custom_call" | custom-call | tf_op jit(solution)/shard_map/pallas_call | solution.py:326
  24.1 1.1 %shard_map.77 = (f32[3,4,128,128]{3,2,1,0:T(8,128)}, f32[4,128,128]{2,1,0:T(8,128)}, f32[4,128,128]{2,1,0:T(8,128)}) custom-call(f32[3,4,128,128]{3,2,1,0:T(8,128)S(1)} %get-tuple-element.6.refs_0_, f32[4,128,128]{2,1,0:T(8,128)S(1)} %get-tuple-element.7.refs_1_, f32[4,128,128]{2,1,0:T(8,128)S(1)} %get-tuple-element.8.refs_2_), custom_call_target="tpu_custom_call" | custom-call | tf_op jit(solution)/shard_map/pallas_call | solution.py:357

commit v3 on v2

--- a/solution.py
+++ b/solution.py
@@ -39,17 +39,20 @@
     sizes,
     data_h, weight_h, ps_h, pm_h, cot_h,
     dual_o, wg_o, dg_o,
-    data, weight, cot, q_all, u, v_m, v_s, hc, gs, aux, wacc, xbuf, tbuf, tile, rcv, pln, spare,
+    data, weight, cot, q_all, u, v_m, v_s, hc, gs, aux, wacc, xbuf, tbuf, rbuf, tile, rcv, pln, spare,
     in_sem, send_sem, recv_sem,
 ):
     pos = tuple(lax.axis_index(a) for a in AXES)
     pm, ps, cm, cs = 0, 1, 2, 3
+    rest = slice(1, NPL)
     loads = (
-        pltpu.make_async_copy(pm_h, q_all.at[pm, :, 1 : NPL + 1, PAD : PAD + NRW], in_sem.at[0]),
-        pltpu.make_async_copy(data_h, data, in_sem.at[1]),
-        pltpu.make_async_copy(ps_h, q_all.at[ps, :, 1 : NPL + 1, PAD : PAD + NRW], in_sem.at[2]),
-        pltpu.make_async_copy(weight_h, weight, in_sem.at[3]),
-        pltpu.make_async_copy(cot_h, cot, in_sem.at[4]),
+        pltpu.make_async_copy(pm_h.at[:, 0], q_all.at[pm, :, 1, PAD : PAD + NRW], in_sem.at[0]),
+        pltpu.make_async_copy(data_h.at[0], data.at[0], in_sem.at[1]),
+        pltpu.make_async_copy(pm_h.at[:, rest], q_all.at[pm, :, 2 : NPL + 1, PAD : PAD + NRW], in_sem.at[2]),
+        pltpu.make_async_copy(data_h.at[rest], data.at[rest], in_sem.at[3]),
+        pltpu.make_async_copy(ps_h, q_all.at[ps, :, 1 : NPL + 1, PAD : PAD + NRW], in_sem.at[4]),
+        pltpu.make_async_copy(weight_h, weight, in_sem.at[5]),
+        pltpu.make_async_copy(cot_h, cot, in_sem.at[6]),
     )
     for c in loads:
         c.start()
@@ -94,7 +97,9 @@
     def message(e, s):
         off, kind = SLOTS[s]
         if kind is None:
-            src = q_all.at[e, 0, NPL, PAD : PAD + NRW] if s == 10 else u.at[e, 0]
+            first = (pm_h.at[0, NPL - 1], ps_h.at[0, NPL - 1], q_all.at[cm, 0, NPL, PAD : PAD + NRW],
+                     q_all.at[cs, 0, NPL, PAD : PAD + NRW])
+            src = first[e] if s == 10 else u.at[e, 0]
             dst, sem = pln.at[e, s - 10], s - 9
         else:
             src, dst, sem = tile.at[e, 8 * kind : 8 * kind + 8], rcv.at[e, s], 0
@@ -125,13 +130,17 @@
         x = jnp.where(lane == k, pltpu.roll(q2, k + 1, 1), xbuf[out])
         xbuf[out] = jnp.where(lane == k + NPL, pltpu.roll(total, k + NPL, 1), x)
 
-    def send_all(e):
+    def send_last_plane(e):
+        pl.when(up_z)(lambda: message(e, 10).start())
+
+    def send_first_plane(e):
+        pl.when(low_z)(lambda: message(e, 11).start())
+
+    def send_tiles(e):
         for j in range(NRW // CH):
             rows = slice(PAD + CH * j, PAD + CH * (j + 1))
             out = slice(CH * j, CH * (j + 1))
             xbuf[out] = jnp.where(lane == 8, pltpu.roll(q_all[e, 0, NPL, rows], 8, 1), xbuf[out])
-        pl.when(up_z)(lambda: message(e, 10).start())
-        pl.when(low_z)(lambda: message(e, 11).start())
         xt = jnp.transpose(xbuf[...])
         tile[e, 16:24] = xt[0:8]
         tile[e, 9:10] = xt[8:9]
@@ -139,45 +148,44 @@
         for k in range(NPL):
             tile[e, k : k + 1] = q_all[e, 1, k + 1, PAD + NRW - 1 : PAD + NRW]
             tile[e, k + NPL : k + NPL + 1] = u[e, k, 0:1]
-        for s in range(10):
+        for s in (6, 7, 8, 9, 2, 3, 4, 5, 0, 1):
             pl.when(takes[s])(lambda: message(e, s).start())
             pl.when(jnp.logical_not(takes[s]))(lambda: filler(e, s, send_sem).start())
             pl.when(jnp.logical_not(has[s]))(lambda: filler(e, s, recv_sem).start())
 
-    def receive(e, v):
+    def receive_tiles(e):
         tiles_done(e, recv_sem)
         low_c = jnp.where(low_y, rcv[e, 2, 0:NPL], 0.0)
         high_c = rcv[e, 3, NPL : 2 * NPL] - tile[e, 16 : 16 + NPL]
         high_c = high_c - jnp.where(jnp.logical_and(sub4 == 0, low_z), rcv[e, 7, 1:2], 0.0)
         high_c = high_c - jnp.where(jnp.logical_and(lane8 == 0, low_x), rcv[e, 9, 0:NPL], 0.0)
-        high_c = jnp.where(up_y, high_c, 0.0)
         tbuf[0:NPL] = low_c
-        tbuf[NPL : 2 * NPL] = high_c
+        tbuf[NPL : 2 * NPL] = jnp.where(up_y, high_c, 0.0)
         tbuf[8:16] = jnp.where(low_y, rcv[e, 6], 0.0)
         tbuf[...] = jnp.transpose(tbuf[...])
-
-        def planes(k, _):
-            for j in range(NRW // CH):
-                out = slice(CH * j, CH * (j + 1))
-                col = pltpu.roll(tbuf[out], NCL - k, 1)
-                v[k, out] = u[e, k, out] - jnp.where(lane == 0, col, 0.0)
-            return 0
-
-        lax.fori_loop(0, NPL, planes, 0)
         high_r = rcv[e, 1, NPL : 2 * NPL] - tile[e, 0:NPL]
         high_r = high_r - jnp.where(jnp.logical_and(sub4 == 0, low_z), rcv[e, 5, 0:1], 0.0)
         high_r = high_r - jnp.where(jnp.logical_and(lane8 == 0, low_y), rcv[e, 8, 0:NPL], 0.0)
-        high_r = jnp.where(up_x, high_r, 0.0)
-        low_r = jnp.where(low_x, rcv[e, 0, 0:NPL], 0.0)
-        for k in range(NPL):
-            v[k, 0:1] = v[k, 0:1] - low_r[k : k + 1]
-            v[k, NRW : NRW + 1] = high_r[k : k + 1]
-        pl.when(low_z)(lambda: message(e, 10).wait_recv())
+        rbuf[0:NPL] = jnp.where(low_x, rcv[e, 0, 0:NPL], 0.0)
+        rbuf[NPL : 2 * NPL] = jnp.where(up_x, high_r, 0.0)
+
+    def fix(e, v, k):
+        if k == 0:
+            pl.when(low_z)(lambda: message(e, 10).wait_recv())
+        for j in range(NRW // CH):
+            out = slice(CH * j, CH * (j + 1))
+            total = u[e, k, out] - jnp.where(lane == 0, pltpu.roll(tbuf[out], (NCL - k) % NCL, 1), 0.0)
+            if k == 0:
+                total = total - pln[e, 0, out]
+            v[k, out] = total
+        v[k, 0:1] = v[k, 0:1] - rbuf[k : k + 1]
+        v[k, NRW : NRW + 1] = rbuf[NPL + k : NPL + k + 1]
+
+    def fix_beyond(e, v):
         pl.when(up_z)(lambda: message(e, 11).wait_recv())
         for j in range(NRW // CH):
             rows = slice(PAD + CH * j, PAD + CH * (j + 1))
             out = slice(CH * j, CH * (j + 1))
-            v[0, out] = v[0, out] - pln[e, 0, out]
             col = jnp.where(lane == 0, pltpu.roll(tbuf[out], NCL - 8, 1), 0.0)
             v[NPL, out] = jnp.where(up_z, pln[e, 1, out] - q_all[e, 0, NPL, rows] - col, 0.0)
         v[NPL, 0:1] = v[NPL, 0:1] - jnp.where(jnp.logical_and(up_z, low_x), rcv[e, 4, 0:1], 0.0)
@@ -192,27 +200,53 @@
             jnp.where(lane == NCL - 1, col, pltpu.roll(c, NCL - 1, 1)) - c,
         )
 
-    def each_chunk(body):
-        def planes(k, _):
-            for j in range(NRW // CH):
-                body(k, j)
-            return 0
-        lax.fori_loop(0, NPL, planes, 0)
+    def plane(body, k):
+        for j in range(NRW // CH):
+            body(k, j)
+
+    def parts(e, k, extra=False):
+        plane(lambda k, j: divide_part(e, k, j, extra), k)
 
     def spots(j):
         return slice(PAD + CH * j, PAD + CH * (j + 1)), slice(CH * j, CH * (j + 1))
 
+    def step(e, v, body, nxt):
+        receive_tiles(e)
+        fix(e, v, 3)
+        fix_beyond(e, v)
+        plane(body, 3)
+        send_last_plane(nxt)
+        fix(e, v, 0)
+        fix(e, v, 1)
+        plane(body, 0)
+        parts(nxt, 0)
+        send_first_plane(nxt)
+        fix(e, v, 2)
+        for k in (1, 2):
+            plane(body, k)
+            parts(nxt, k)
+        parts(nxt, 3)
+        send_tiles(nxt)
+
+    send_last_plane(pm)
     loads[0].wait()
     loads[1].wait()
-    each_chunk(lambda k, j: divide_part(pm, k, j, True))
-    send_all(pm)
+    parts(pm, 0, True)
+    send_first_plane(pm)
     loads[2].wait()
-    each_chunk(lambda k, j: divide_part(ps, k, j, True))
-    send_all(ps)
     loads[3].wait()
+    for k in range(1, NPL):
+        parts(pm, k, True)
+    send_tiles(pm)
+    send_last_plane(ps)
     loads[4].wait()
-
-    receive(pm, v_m)
+    parts(ps, 0, True)
+    send_first_plane(ps)
+    for k in range(1, NPL):
+        parts(ps, k, True)
+    send_tiles(ps)
+    loads[5].wait()
+    loads[6].wait()
 
     def adjoint_mid(k, j):
         rows, out = spots(j)
@@ -235,12 +269,13 @@
             hc_a = h * c[a]
             hc[a, k, out] = hc_a
             q_all[cm, a, k + 1, rows] = TAU * hc_a - f * g[a]
-        divide_part(cm, k, j, False)
-
-    each_chunk(adjoint_mid)
-    send_all(cm)
-
-    receive(ps, v_s)
+
+    step(pm, v_m, adjoint_mid, cm)
+
+    receive_tiles(ps)
+    for k in range(NPL):
+        fix(ps, v_s, k)
+    fix_beyond(ps, v_s)
 
     def prepare_start(k, j):
         rows, out = spots(j)
@@ -258,9 +293,8 @@
         for a in range(3):
             gs[a, k, out] = g[a]
 
-    each_chunk(prepare_start)
-
-    receive(cm, v_m)
+    for k in range(NPL):
+        plane(prepare_start, k)
 
     def adjoint_start(k, j):
         rows, out = spots(j)
@@ -278,17 +312,16 @@
             hc_a = h * c[a]
             hc[a, k, out] = hc_a
             q_all[cs, a, k + 1, rows] = TAU * hc_a - f * g[a]
-        divide_part(cs, k, j, False)
-
-    each_chunk(adjoint_start)
-    send_all(cs)
+
+    step(cm, v_m, adjoint_start, cs)
 
     def finish_weight(k, j):
         _, out = spots(j)
         wg_o[k, out] = wacc[k, out] / weight[k, out]
 
-    each_chunk(finish_weight)
-    receive(cs, v_s)
+    for k in range(NPL):
+        plane(finish_weight, k)
+    receive_tiles(cs)
 
     def finish(k, j):
         _, out = spots(j)
@@ -297,7 +330,14 @@
             dual_o[a, k, out] = hc[a, k, out] + d[a]
         dg_o[k, out] = KAPPA * (v_s[k, out] + v_m[k, out])
 
-    each_chunk(finish)
+    for k in (1, 2, 3):
+        fix(cs, v_s, k)
+    plane(finish, 1)
+    plane(finish, 2)
+    fix(cs, v_s, 0)
+    plane(finish, 0)
+    fix_beyond(cs, v_s)
+    plane(finish, 3)
     for e in range(4):
         tiles_done(e, send_sem)
         pl.when(up_z)(lambda: message(e, 10).wait_send())
@@ -342,11 +382,12 @@
             vm(field, F32),
             vm((NRW, NCL), F32),
             vm((NRW, NCL), F32),
+            vm((8, NCL), F32),
             vm((4, 24, NCL), F32),
             vm((4, 10, 8, NCL), F32),
             vm((4, 2, NRW, NCL), F32),
             vm((4, 10, 8, NCL), F32),
-            pltpu.SemaphoreType.DMA((5,)),
+            pltpu.SemaphoreType.DMA((7,)),
             pltpu.SemaphoreType.DMA((4, 3)),
             pltpu.SemaphoreType.DMA((4, 3)),
         ],

time: 25.3 us -> 22.7 us (0.90)
  Pallas kernels: 24.5 us -> 21.9 us
    pallas_call x1, Pallas kernels: 23.5 us -> 20.8 us  [shards(): pl.pallas_call(functools.partial(kernel, sizes), out_shape=shapes, in_spe...]
where the time goes in v3:
time: 22.7 us; the launch traced here: 22.6 us
  Pallas kernels  21.9 us (96%)
  between operations  0.64 us (3%)
    pallas_call x1, Pallas kernels, shards(): pl.pallas_call(functools.partial(kernel, sizes), out_shape=shapes, in_spe...  20.8 us
    pallas_call x1, Pallas kernels, shards(): pl.pallas_call(write_out, out_shape=shapes, in_specs=[pl.BlockSpec(memory...  1.08 us

profile of v3, /device:TPU:103, one launch (start us, length us, event | category | flops | bytes accessed | tf_op | source)
XLA Modules:
  0.0 22.6 jit_solution(7498994604129097972)
XLA Ops:
  0.6 20.8 %shard_map.76 = (f32[3,4,128,128]{3,2,1,0:T(8,128)S(1)}, f32[4,128,128]{2,1,0:T(8,128)S(1)}, f32[4,128,128]{2,1,0:T(8,128)S(1)}) custom-call(f32[4,128,128]{2,1,0:T(8,128)} %data_h.1, f32[4,128,128]{2,1,0:T(8,128)} %weight_h.1, f32[3,4,128,128]{3,2,1,0:T(8,128)} %ps_h.1, f32[3,4,128,128]{3,2,1,0:T(8,128)} %pm_h.1, f32[3,4,128,128]{3,2,1,0:T(8,128)} %cot_h.1), custom_call_target="tpu_custom_call" | custom-call | tf_op jit(solution)/shard_map/pallas_call | solution.py:366
  21.5 1.1 %shard_map.77 = (f32[3,4,128,128]{3,2,1,0:T(8,128)}, f32[4,128,128]{2,1,0:T(8,128)}, f32[4,128,128]{2,1,0:T(8,128)}) custom-call(f32[3,4,128,128]{3,2,1,0:T(8,128)S(1)} %get-tuple-element.6.refs_0_, f32[4,128,128]{2,1,0:T(8,128)S(1)} %get-tuple-element.7.refs_1_, f32[4,128,128]{2,1,0:T(8,128)S(1)} %get-tuple-element.8.refs_2_), custom_call_target="tpu_custom_call" | custom-call | tf_op jit(solution)/shard_map/pallas_call | solution.py:398

commit v4 on v3

--- a/solution.py
+++ b/solution.py
@@ -38,22 +38,20 @@
 def kernel(
     sizes,
     data_h, weight_h, ps_h, pm_h, cot_h,
-    dual_o, wg_o, dg_o,
-    data, weight, cot, q_all, u, v_m, v_s, hc, gs, aux, wacc, xbuf, tbuf, rbuf, tile, rcv, pln, spare,
+    hc_o, wg_o, u_o, dm_o, t_o, r_o, edge_o,
+    data, weight, cot, q_all, u, v_m, v_s, gs, bs, aux, wacc, scale, inner, xbuf, tbuf, rbuf, tile, rcv, pln, spare,
     in_sem, send_sem, recv_sem,
 ):
     pos = tuple(lax.axis_index(a) for a in AXES)
     pm, ps, cm, cs = 0, 1, 2, 3
     rest = slice(1, NPL)
-    loads = (
-        pltpu.make_async_copy(pm_h.at[:, 0], q_all.at[pm, :, 1, PAD : PAD + NRW], in_sem.at[0]),
-        pltpu.make_async_copy(data_h.at[0], data.at[0], in_sem.at[1]),
-        pltpu.make_async_copy(pm_h.at[:, rest], q_all.at[pm, :, 2 : NPL + 1, PAD : PAD + NRW], in_sem.at[2]),
-        pltpu.make_async_copy(data_h.at[rest], data.at[rest], in_sem.at[3]),
-        pltpu.make_async_copy(ps_h, q_all.at[ps, :, 1 : NPL + 1, PAD : PAD + NRW], in_sem.at[4]),
-        pltpu.make_async_copy(weight_h, weight, in_sem.at[5]),
-        pltpu.make_async_copy(cot_h, cot, in_sem.at[6]),
-    )
+    loads = [
+        pltpu.make_async_copy(pm_h, q_all.at[pm, :, 1 : NPL + 1, PAD : PAD + NRW], in_sem.at[0]),
+        pltpu.make_async_copy(data_h, data, in_sem.at[1]),
+    ]
+    loads.append(pltpu.make_async_copy(ps_h, q_all.at[ps, :, 1 : NPL + 1, PAD : PAD + NRW], in_sem.at[2]))
+    loads.append(pltpu.make_async_copy(weight_h, weight, in_sem.at[3]))
+    loads.append(pltpu.make_async_copy(cot_h, cot, in_sem.at[4]))
     for c in loads:
         c.start()
 
@@ -92,7 +90,6 @@
         for k in range(NPL):
             q_all[e, 1, k + 1, 0:PAD] = jnp.zeros((PAD, NCL), F32)
 
-    pl.semaphore_wait(barrier, sum(jnp.where(here, 1, 0) for here in has))
 
     def message(e, s):
         off, kind = SLOTS[s]
@@ -136,7 +133,7 @@
     def send_first_plane(e):
         pl.when(low_z)(lambda: message(e, 11).start())
 
-    def send_tiles(e):
+    def pack_tiles(e):
         for j in range(NRW // CH):
             rows = slice(PAD + CH * j, PAD + CH * (j + 1))
             out = slice(CH * j, CH * (j + 1))
@@ -148,6 +145,7 @@
         for k in range(NPL):
             tile[e, k : k + 1] = q_all[e, 1, k + 1, PAD + NRW - 1 : PAD + NRW]
             tile[e, k + NPL : k + NPL + 1] = u[e, k, 0:1]
+    def send_tiles(e):
         for s in (6, 7, 8, 9, 2, 3, 4, 5, 0, 1):
             pl.when(takes[s])(lambda: message(e, s).start())
             pl.when(jnp.logical_not(takes[s]))(lambda: filler(e, s, send_sem).start())
@@ -226,49 +224,61 @@
             plane(body, k)
             parts(nxt, k)
         parts(nxt, 3)
+        pack_tiles(nxt)
         send_tiles(nxt)
 
+    for k in range(NPL):
+        if k == 0:
+            loads[0].wait()
+            loads[1].wait()
+        parts(pm, k, True)
+    pack_tiles(pm)
+    pl.semaphore_wait(barrier, sum(jnp.where(here, 1, 0) for here in has))
     send_last_plane(pm)
-    loads[0].wait()
-    loads[1].wait()
-    parts(pm, 0, True)
     send_first_plane(pm)
-    loads[2].wait()
-    loads[3].wait()
-    for k in range(1, NPL):
-        parts(pm, k, True)
     send_tiles(pm)
     send_last_plane(ps)
-    loads[4].wait()
+    loads[2].wait()
     parts(ps, 0, True)
     send_first_plane(ps)
     for k in range(1, NPL):
         parts(ps, k, True)
+    pack_tiles(ps)
     send_tiles(ps)
-    loads[5].wait()
-    loads[6].wait()
+    loads[3].wait()
+    loads[4].wait()
+
+    def multiply_mid(k, j):
+        rows, out = spots(j)
+        s = None
+        for a in range(3):
+            term = cot[a, k, out] * q_all[pm, a, k + 1, rows]
+            s = term if s is None else s + term
+        inner[k, out] = s
+
+    for k in range(NPL):
+        plane(multiply_mid, k)
+
+    def weights(g, w):
+        t = g[0] * g[0] + g[1] * g[1] + g[2] * g[2] + DELTA
+        rn = lax.rsqrt(t)
+        n = t * rn
+        r = 1.0 / (w + TAU * n)
+        return rn, n, w * r, TAU * r
 
     def adjoint_mid(k, j):
         rows, out = spots(j)
         g = slopes(v_m, k, j)
-        t = g[0] * g[0] + g[1] * g[1] + g[2] * g[2] + DELTA
-        rn = lax.rsqrt(t)
-        n = t * rn
-        w = weight[k, out]
-        r = 1.0 / (w + TAU * n)
-        h = w * r
+        rn, n, h, tr = weights(g, weight[k, out])
         c = [cot[a, k, out] for a in range(3)]
-        s = None
-        for a in range(3):
-            term = c[a] * (q_all[pm, a, k + 1, rows] + TAU * g[a])
-            s = term if s is None else s + term
-        m = TAU * r * (h * s)
+        s = inner[k, out] + TAU * (c[0] * g[0] + c[1] * g[1] + c[2] * g[2])
+        m = tr * (h * s)
+        f = m * rn
+        th = TAU * h
+        for a in range(3):
+            q_all[cm, a, k + 1, rows] = th * c[a] - f * g[a]
         wacc[k, out] = m * n
-        f = m * rn
-        for a in range(3):
-            hc_a = h * c[a]
-            hc[a, k, out] = hc_a
-            q_all[cm, a, k + 1, rows] = TAU * hc_a - f * g[a]
+        scale[k, out] = h
 
     step(pm, v_m, adjoint_mid, cm)
 
@@ -279,19 +289,18 @@
 
     def prepare_start(k, j):
         rows, out = spots(j)
+        for a in range(3):
+            hc_o[a, k, out] = scale[k, out] * cot[a, k, out]
         g = slopes(v_s, k, j)
-        t = g[0] * g[0] + g[1] * g[1] + g[2] * g[2] + DELTA
-        rn = lax.rsqrt(t)
-        n = t * rn
-        w = weight[k, out]
-        r = 1.0 / (w + TAU * n)
-        h = w * r
-        a1 = TAU * r * h
-        aux[0, k, out] = h
+        rn, n, h, tr = weights(g, weight[k, out])
+        a1 = tr * h
+        aux[0, k, out] = TAU * h
         aux[1, k, out] = a1 * rn
         aux[2, k, out] = a1 * n
+        scale[k, out] = h
         for a in range(3):
             gs[a, k, out] = g[a]
+            bs[a, k, out] = q_all[ps, a, k + 1, rows] + TAU * g[a]
 
     for k in range(NPL):
         plane(prepare_start, k)
@@ -299,56 +308,69 @@
     def adjoint_start(k, j):
         rows, out = spots(j)
         d = slopes(v_m, k, j)
-        h = aux[0, k, out]
-        g = [gs[a, k, out] for a in range(3)]
-        c = [hc[a, k, out] + d[a] for a in range(3)]
-        s = None
-        for a in range(3):
-            term = c[a] * (q_all[ps, a, k + 1, rows] + TAU * g[a])
-            s = term if s is None else s + term
-        wacc[k, out] = wacc[k, out] + aux[2, k, out] * s
+        c = [hc_o[a, k, out] + d[a] for a in range(3)]
+        s = c[0] * bs[0, k, out] + c[1] * bs[1, k, out] + c[2] * bs[2, k, out]
         f = aux[1, k, out] * s
-        for a in range(3):
-            hc_a = h * c[a]
-            hc[a, k, out] = hc_a
-            q_all[cs, a, k + 1, rows] = TAU * hc_a - f * g[a]
+        th = aux[0, k, out]
+        for a in range(3):
+            q_all[cs, a, k + 1, rows] = th * c[a] - f * gs[a, k, out]
+            hc_o[a, k, out] = c[a]
+        inner[k, out] = s
 
     step(cm, v_m, adjoint_start, cs)
 
     def finish_weight(k, j):
         _, out = spots(j)
-        wg_o[k, out] = wacc[k, out] / weight[k, out]
+        wg_o[k, out] = (wacc[k, out] + aux[2, k, out] * inner[k, out]) / weight[k, out]
+        for a in range(3):
+            hc_o[a, k, out] = scale[k, out] * hc_o[a, k, out]
+        dm_o[k, out] = v_m[k, out]
+        u_o[k, out] = u[cs, k, out]
 
     for k in range(NPL):
         plane(finish_weight, k)
     receive_tiles(cs)
-
-    def finish(k, j):
-        _, out = spots(j)
-        d = slopes(v_s, k, j)
-        for a in range(3):
-            dual_o[a, k, out] = hc[a, k, out] + d[a]
-        dg_o[k, out] = KAPPA * (v_s[k, out] + v_m[k, out])
-
-    for k in (1, 2, 3):
-        fix(cs, v_s, k)
-    plane(finish, 1)
-    plane(finish, 2)
-    fix(cs, v_s, 0)
-    plane(finish, 0)
+    t_o[...] = tbuf[...]
+    r_o[...] = rbuf[...]
     fix_beyond(cs, v_s)
-    plane(finish, 3)
+    edge_o[1] = v_s[NPL, 0:NRW]
+    pl.when(low_z)(lambda: message(cs, 10).wait_recv())
+    edge_o[0] = pln[cs, 0]
     for e in range(4):
         tiles_done(e, send_sem)
         pl.when(up_z)(lambda: message(e, 10).wait_send())
         pl.when(low_z)(lambda: message(e, 11).wait_send())
 
 
-def write_out(*refs):
-    sem = refs[-1]
-    copies = [pltpu.make_async_copy(refs[i], refs[i + 3], sem.at[i]) for i in range(3)]
-    for c in copies:
-        c.start()
+def finish(hc, wg, u, dm, tcol, rrow, edge, dual_h, wg_h, dg_h, v, dual, dg, sem):
+    lane = lax.broadcasted_iota(jnp.int32, (CH, NCL), 1)
+    copies = [pltpu.make_async_copy(wg, wg_h, sem.at[0])]
+    copies[0].start()
+    v[NPL, 0:NRW] = edge[1]
+    for k in reversed(range(NPL)):
+        for j in range(NRW // CH):
+            out = slice(CH * j, CH * (j + 1))
+            total = u[k, out] - jnp.where(lane == 0, pltpu.roll(tcol[out], (NCL - k) % NCL, 1), 0.0)
+            if k == 0:
+                total = total - edge[0, out]
+            v[k, out] = total
+        v[k, 0:1] = v[k, 0:1] - rrow[k : k + 1]
+        v[k, NRW : NRW + 1] = rrow[NPL + k : NPL + k + 1]
+        for j in range(NRW // CH):
+            out = slice(CH * j, CH * (j + 1))
+            c = v[k, out]
+            col = pltpu.roll(tcol[out], NCL - 1 - NPL - k, 1)
+            dual[0, k, out] = hc[0, k, out] + (v[k + 1, out] - c)
+            dual[1, k, out] = hc[1, k, out] + (v[k, CH * j + 1 : CH * (j + 1) + 1] - c)
+            dual[2, k, out] = hc[2, k, out] + (jnp.where(lane == NCL - 1, col, pltpu.roll(c, NCL - 1, 1)) - c)
+            dg[k, out] = KAPPA * (c + dm[k, out])
+        here = [
+            pltpu.make_async_copy(dual.at[:, k], dual_h.at[:, k], sem.at[2 * k + 1]),
+            pltpu.make_async_copy(dg.at[k], dg_h.at[k], sem.at[2 * k + 2]),
+        ]
+        for c in here:
+            c.start()
+        copies += here
     for c in copies:
         c.wait()
 
@@ -363,11 +385,13 @@
         jax.ShapeDtypeStruct(field, F32),
     )
     args = (data, weight, dual_start, dual_mid, cotangent)
+    face = (NRW, NCL)
+    between = ((3,) + field, field, field, field, face, (8, NCL), (2,) + face)
     results = pl.pallas_call(
         functools.partial(kernel, sizes),
-        out_shape=shapes,
+        out_shape=[jax.ShapeDtypeStruct(x, F32) for x in between],
         in_specs=[pl.BlockSpec(memory_space=pl.ANY)] * 5,
-        out_specs=(whole,) * 3,
+        out_specs=[whole] * len(between),
         scratch_shapes=[
             vm(field, F32),
             vm(field, F32),
@@ -380,6 +404,8 @@
             vm((3,) + field, F32),
             vm((3,) + field, F32),
             vm(field, F32),
+            vm(field, F32),
+            vm(field, F32),
             vm((NRW, NCL), F32),
             vm((NRW, NCL), F32),
             vm((8, NCL), F32),
@@ -387,7 +413,7 @@
             vm((4, 10, 8, NCL), F32),
             vm((4, 2, NRW, NCL), F32),
             vm((4, 10, 8, NCL), F32),
-            pltpu.SemaphoreType.DMA((7,)),
+            pltpu.SemaphoreType.DMA((5,)),
             pltpu.SemaphoreType.DMA((4, 3)),
             pltpu.SemaphoreType.DMA((4, 3)),
         ],
@@ -396,11 +422,16 @@
         ),
     )(*[pltpu.with_memory_space_constraint(x, pltpu.HBM) for x in args])
     return pl.pallas_call(
-        write_out,
+        finish,
         out_shape=shapes,
-        in_specs=[pl.BlockSpec(memory_space=pltpu.VMEM)] * 3,
+        in_specs=[whole] * len(between),
         out_specs=(pl.BlockSpec(memory_space=pl.ANY),) * 3,
-        scratch_shapes=[pltpu.SemaphoreType.DMA((3,))],
+        scratch_shapes=[
+            vm((NPL + 1, NRW + PAD, NCL), F32),
+            vm((3,) + field, F32),
+            vm(field, F32),
+            pltpu.SemaphoreType.DMA((9,)),
+        ],
     )(*[pltpu.with_memory_space_constraint(x, pltpu.VMEM) for x in results])
 
 

time: 22.7 us -> 22.2 us (0.978)
  Pallas kernels: 21.9 us -> 21.4 us
    pallas_call x2, Pallas kernels: 21.9 us -> 21.4 us  [the longest x1 20.2 us: shards(): pl.pallas_call(functools.partial(kernel, sizes), out_shape=[jax.ShapeDtyp...]
where the time goes in v4:
time: 22.2 us; the launch traced here: 22.1 us
  Pallas kernels  21.4 us (96%)
  between operations  0.64 us (3%)
    pallas_call x1, Pallas kernels, shards(): pl.pallas_call(functools.partial(kernel, sizes), out_shape=[jax.ShapeDtyp...  20.2 us
    pallas_call x1, Pallas kernels, shards(): pl.pallas_call(finish, out_shape=shapes, in_specs=[whole] * len(between),...  1.23 us

profile of v4, /device:TPU:103, one launch (start us, length us, event | category | flops | bytes accessed | tf_op | source)
XLA Modules:
  0.0 22.1 jit_solution(1049489986477000291)
XLA Ops:
  0.6 20.2 %shard_map.76 = (f32[3,4,128,128]{3,2,1,0:T(8,128)S(1)}, f32[4,128,128]{2,1,0:T(8,128)S(1)}, f32[4,128,128]{2,1,0:T(8,128)S(1)}, f32[4,128,128]{2,1,0:T(8,128)S(...) custom-call(f32[4,128,128]{2,1,0:T(8,128)} %data_h.1, f32[4,128,128]{2,1,0:T(8,128)} %weight_h.1, ...), custom_call_target="tpu_custom_call" | custom-call | tf_op jit(solution)/shard_map/pallas_call | solution.py:390
  20.8 1.2 %shard_map.77 = (f32[3,4,128,128]{3,2,1,0:T(8,128)}, f32[4,128,128]{2,1,0:T(8,128)}, f32[4,128,128]{2,1,0:T(8,128)}) custom-call(f32[3,4,128,128]{3,2,1,0:T(8,128)S(1)} %get-tuple-element.10.hc, f32[4,128,128]{2,1,0:T(8,128)S(1)} %get-tuple-element.11.wg, f32[4,128,128]{2,1,0:T(8,128)S(1)} %get-tuple-element.12.u, f32[4,128,128]{2,1,0:T(8,128)S(1)} %get-tuple-element.13.dm, ...), custom_call_target="tpu_custom_call" | custom-call | tf_op jit(solution)/shard_map/pallas_call | solution.py:424

commit v5 on v4

--- a/solution.py
+++ b/solution.py
@@ -39,7 +39,7 @@
     sizes,
     data_h, weight_h, ps_h, pm_h, cot_h,
     hc_o, wg_o, u_o, dm_o, t_o, r_o, edge_o,
-    data, weight, cot, q_all, u, v_m, v_s, gs, bs, aux, wacc, scale, inner, xbuf, tbuf, rbuf, tile, rcv, pln, spare,
+    data, weight, cot, q_all, u, v_m, v_s, gs, bs, aux, wacc, scale, inner, xbuf, tbuf, cols, rbuf, tile, rcv, pln, spare,
     in_sem, send_sem, recv_sem,
 ):
     pos = tuple(lax.axis_index(a) for a in AXES)
@@ -56,8 +56,9 @@
         c.start()
 
     lane = lax.broadcasted_iota(jnp.int32, (CH, NCL), 1)
-    lane8 = lax.broadcasted_iota(jnp.int32, (NPL, NCL), 1)
-    sub4 = lax.broadcasted_iota(jnp.int32, (NPL, NCL), 0)
+    lane8 = lax.broadcasted_iota(jnp.int32, (8, NCL), 1)
+    sub8 = lax.broadcasted_iota(jnp.int32, (8, NCL), 0)
+    odd = sub8 % 2 == 1
 
     low_x, low_y, low_z = (p > 0 for p in pos)
     up_x, up_y, up_z = (p < n - 1 for p, n in zip(pos, sizes))
@@ -124,8 +125,8 @@
         if extra:
             total = total - KAPPA * data[k, out]
         u[e, k, out] = total
-        x = jnp.where(lane == k, pltpu.roll(q2, k + 1, 1), xbuf[out])
-        xbuf[out] = jnp.where(lane == k + NPL, pltpu.roll(total, k + NPL, 1), x)
+        ends = pltpu.roll(jnp.where(lane < NCL // 2, total, q2), 2 * k + 1, 1)
+        xbuf[out] = jnp.where(lane // 2 == k, ends, xbuf[out])
 
     def send_last_plane(e):
         pl.when(up_z)(lambda: message(e, 10).start())
@@ -143,8 +144,8 @@
         tile[e, 9:10] = xt[8:9]
         tile[e, 8:9] = q_all[e, 0, NPL, PAD : PAD + 1]
         for k in range(NPL):
-            tile[e, k : k + 1] = q_all[e, 1, k + 1, PAD + NRW - 1 : PAD + NRW]
-            tile[e, k + NPL : k + NPL + 1] = u[e, k, 0:1]
+            tile[e, 2 * k : 2 * k + 1] = q_all[e, 1, k + 1, PAD + NRW - 1 : PAD + NRW]
+            tile[e, 2 * k + 1 : 2 * k + 2] = u[e, k, 0:1]
     def send_tiles(e):
         for s in (6, 7, 8, 9, 2, 3, 4, 5, 0, 1):
             pl.when(takes[s])(lambda: message(e, s).start())
@@ -153,34 +154,38 @@
 
     def receive_tiles(e):
         tiles_done(e, recv_sem)
-        low_c = jnp.where(low_y, rcv[e, 2, 0:NPL], 0.0)
-        high_c = rcv[e, 3, NPL : 2 * NPL] - tile[e, 16 : 16 + NPL]
-        high_c = high_c - jnp.where(jnp.logical_and(sub4 == 0, low_z), rcv[e, 7, 1:2], 0.0)
-        high_c = high_c - jnp.where(jnp.logical_and(lane8 == 0, low_x), rcv[e, 9, 0:NPL], 0.0)
-        tbuf[0:NPL] = low_c
-        tbuf[NPL : 2 * NPL] = jnp.where(up_y, high_c, 0.0)
+        high_c = pltpu.roll(rcv[e, 3], 7, 0) - tile[e, 16:24]
+        high_c = high_c - jnp.where(jnp.logical_and(sub8 == 0, low_z), rcv[e, 7, 1:2], 0.0)
+        high_c = high_c - jnp.where(jnp.logical_and(lane8 == 0, low_x), rcv[e, 9], 0.0)
+        high_c = jnp.where(up_y, high_c, 0.0)
+        low_c = jnp.where(low_y, pltpu.roll(rcv[e, 2], 1, 0), 0.0)
+        tbuf[0:8] = jnp.where(odd, low_c, high_c)
         tbuf[8:16] = jnp.where(low_y, rcv[e, 6], 0.0)
         tbuf[...] = jnp.transpose(tbuf[...])
-        high_r = rcv[e, 1, NPL : 2 * NPL] - tile[e, 0:NPL]
-        high_r = high_r - jnp.where(jnp.logical_and(sub4 == 0, low_z), rcv[e, 5, 0:1], 0.0)
-        high_r = high_r - jnp.where(jnp.logical_and(lane8 == 0, low_y), rcv[e, 8, 0:NPL], 0.0)
-        rbuf[0:NPL] = jnp.where(low_x, rcv[e, 0, 0:NPL], 0.0)
-        rbuf[NPL : 2 * NPL] = jnp.where(up_x, high_r, 0.0)
+        high_r = pltpu.roll(rcv[e, 1], 7, 0) - tile[e, 0:8]
+        high_r = high_r - jnp.where(jnp.logical_and(sub8 == 0, low_z), rcv[e, 5, 0:1], 0.0)
+        high_r = high_r - jnp.where(jnp.logical_and(lane8 == 0, low_y), rcv[e, 8], 0.0)
+        high_r = jnp.where(up_x, high_r, 0.0)
+        low_r = jnp.where(low_x, pltpu.roll(rcv[e, 0], 1, 0), 0.0)
+        rbuf[...] = jnp.where(odd, low_r, high_r)
+
+    def receive_planes(e):
+        pl.when(low_z)(lambda: message(e, 10).wait_recv())
+        pl.when(up_z)(lambda: message(e, 11).wait_recv())
 
     def fix(e, v, k):
-        if k == 0:
-            pl.when(low_z)(lambda: message(e, 10).wait_recv())
         for j in range(NRW // CH):
             out = slice(CH * j, CH * (j + 1))
-            total = u[e, k, out] - jnp.where(lane == 0, pltpu.roll(tbuf[out], (NCL - k) % NCL, 1), 0.0)
+            col = pltpu.roll(tbuf[out], NCL - 2 * k - 1, 1)
+            cols[k, out] = col
+            total = u[e, k, out] - jnp.where(lane == 0, col, 0.0)
             if k == 0:
                 total = total - pln[e, 0, out]
             v[k, out] = total
-        v[k, 0:1] = v[k, 0:1] - rbuf[k : k + 1]
-        v[k, NRW : NRW + 1] = rbuf[NPL + k : NPL + k + 1]
+        v[k, 0:1] = v[k, 0:1] - rbuf[2 * k + 1 : 2 * k + 2]
+        v[k, NRW : NRW + 1] = rbuf[2 * k : 2 * k + 1]
 
     def fix_beyond(e, v):
-        pl.when(up_z)(lambda: message(e, 11).wait_recv())
         for j in range(NRW // CH):
             rows = slice(PAD + CH * j, PAD + CH * (j + 1))
             out = slice(CH * j, CH * (j + 1))
@@ -191,7 +196,7 @@
     def slopes(v, k, j):
         out = slice(CH * j, CH * (j + 1))
         c = v[k, out]
-        col = pltpu.roll(tbuf[out], NCL - 1 - NPL - k, 1)
+        col = cols[k, out]
         return (
             v[k + 1, out] - c,
             v[k, CH * j + 1 : CH * (j + 1) + 1] - c,
@@ -210,15 +215,16 @@
 
     def step(e, v, body, nxt):
         receive_tiles(e)
+        receive_planes(e)
         fix(e, v, 3)
+        fix(e, v, 1)
+        fix(e, v, 0)
         fix_beyond(e, v)
         plane(body, 3)
-        send_last_plane(nxt)
-        fix(e, v, 0)
-        fix(e, v, 1)
         plane(body, 0)
         parts(nxt, 0)
         send_first_plane(nxt)
+        send_last_plane(nxt)
         fix(e, v, 2)
         for k in (1, 2):
             plane(body, k)
@@ -283,6 +289,7 @@
     step(pm, v_m, adjoint_mid, cm)
 
     receive_tiles(ps)
+    receive_planes(ps)
     for k in range(NPL):
         fix(ps, v_s, k)
     fix_beyond(ps, v_s)
@@ -330,11 +337,11 @@
     for k in range(NPL):
         plane(finish_weight, k)
     receive_tiles(cs)
+    receive_planes(cs)
     t_o[...] = tbuf[...]
     r_o[...] = rbuf[...]
     fix_beyond(cs, v_s)
     edge_o[1] = v_s[NPL, 0:NRW]
-    pl.when(low_z)(lambda: message(cs, 10).wait_recv())
     edge_o[0] = pln[cs, 0]
     for e in range(4):
         tiles_done(e, send_sem)
@@ -350,16 +357,16 @@
     for k in reversed(range(NPL)):
         for j in range(NRW // CH):
             out = slice(CH * j, CH * (j + 1))
-            total = u[k, out] - jnp.where(lane == 0, pltpu.roll(tcol[out], (NCL - k) % NCL, 1), 0.0)
+            total = u[k, out] - jnp.where(lane == 0, pltpu.roll(tcol[out], NCL - 2 * k - 1, 1), 0.0)
             if k == 0:
                 total = total - edge[0, out]
             v[k, out] = total
-        v[k, 0:1] = v[k, 0:1] - rrow[k : k + 1]
-        v[k, NRW : NRW + 1] = rrow[NPL + k : NPL + k + 1]
+        v[k, 0:1] = v[k, 0:1] - rrow[2 * k + 1 : 2 * k + 2]
+        v[k, NRW : NRW + 1] = rrow[2 * k : 2 * k + 1]
         for j in range(NRW // CH):
             out = slice(CH * j, CH * (j + 1))
             c = v[k, out]
-            col = pltpu.roll(tcol[out], NCL - 1 - NPL - k, 1)
+            col = pltpu.roll(tcol[out], NCL - 2 * k - 1, 1)
             dual[0, k, out] = hc[0, k, out] + (v[k + 1, out] - c)
             dual[1, k, out] = hc[1, k, out] + (v[k, CH * j + 1 : CH * (j + 1) + 1] - c)
             dual[2, k, out] = hc[2, k, out] + (jnp.where(lane == NCL - 1, col, pltpu.roll(c, NCL - 1, 1)) - c)
@@ -408,6 +415,7 @@
             vm(field, F32),
             vm((NRW, NCL), F32),
             vm((NRW, NCL), F32),
+            vm(field, F32),
             vm((8, NCL), F32),
             vm((4, 24, NCL), F32),
             vm((4, 10, 8, NCL), F32),

time: 22.2 us -> 21.8 us (0.982)
  Pallas kernels: 21.4 us -> 21 us
    pallas_call x1, Pallas kernels: 20.2 us -> 19.8 us  [shards(): pl.pallas_call(functools.partial(kernel, sizes), out_shape=[jax.ShapeDtyp...]
where the time goes in v5:
time: 21.8 us; the launch traced here: 21.7 us
  Pallas kernels  21 us (96%)
  between operations  0.64 us (3%)
    pallas_call x1, Pallas kernels, shards(): pl.pallas_call(functools.partial(kernel, sizes), out_shape=[jax.ShapeDtyp...  19.8 us
    pallas_call x1, Pallas kernels, shards(): pl.pallas_call(finish, out_shape=shapes, in_specs=[whole] * len(between),...  1.22 us

profile of v5, /device:TPU:103, one launch (start us, length us, event | category | flops | bytes accessed | tf_op | source)
XLA Modules:
  0.0 21.7 jit_solution(6601272673009439665)
XLA Ops:
  0.6 19.8 %shard_map.76 = (f32[3,4,128,128]{3,2,1,0:T(8,128)S(1)}, f32[4,128,128]{2,1,0:T(8,128)S(1)}, f32[4,128,128]{2,1,0:T(8,128)S(1)}, f32[4,128,128]{2,1,0:T(8,128)S(...) custom-call(f32[4,128,128]{2,1,0:T(8,128)} %data_h.1, f32[4,128,128]{2,1,0:T(8,128)} %weight_h.1, ...), custom_call_target="tpu_custom_call" | custom-call | tf_op jit(solution)/shard_map/pallas_call | solution.py:397
  20.5 1.2 %shard_map.77 = (f32[3,4,128,128]{3,2,1,0:T(8,128)}, f32[4,128,128]{2,1,0:T(8,128)}, f32[4,128,128]{2,1,0:T(8,128)}) custom-call(f32[3,4,128,128]{3,2,1,0:T(8,128)S(1)} %get-tuple-element.10.hc, f32[4,128,128]{2,1,0:T(8,128)S(1)} %get-tuple-element.11.wg, f32[4,128,128]{2,1,0:T(8,128)S(1)} %get-tuple-element.12.u, f32[4,128,128]{2,1,0:T(8,128)S(1)} %get-tuple-element.13.dm, ...), custom_call_target="tpu_custom_call" | custom-call | tf_op jit(solution)/shard_map/pallas_call | solution.py:432

commit v6 on v5

--- a/solution.py
+++ b/solution.py
@@ -14,7 +14,7 @@
 AXES = ("gx", "gy", "gz")
 
 NPL, NRW, NCL = 4, 128, 128
-CH = 32
+CH = 64
 PAD = 8
 R, Z, C = 0, 1, 2
 SLOTS = (
@@ -56,6 +56,7 @@
         c.start()
 
     lane = lax.broadcasted_iota(jnp.int32, (CH, NCL), 1)
+    row = lax.broadcasted_iota(jnp.int32, (CH, NCL), 0)
     lane8 = lax.broadcasted_iota(jnp.int32, (8, NCL), 1)
     sub8 = lax.broadcasted_iota(jnp.int32, (8, NCL), 0)
     odd = sub8 % 2 == 1
@@ -181,8 +182,9 @@
             total = u[e, k, out] - jnp.where(lane == 0, col, 0.0)
             if k == 0:
                 total = total - pln[e, 0, out]
+            if j == 0:
+                total = total - jnp.where(row == 0, rbuf[2 * k + 1 : 2 * k + 2], 0.0)
             v[k, out] = total
-        v[k, 0:1] = v[k, 0:1] - rbuf[2 * k + 1 : 2 * k + 2]
         v[k, NRW : NRW + 1] = rbuf[2 * k : 2 * k + 1]
 
     def fix_beyond(e, v):
@@ -190,8 +192,10 @@
             rows = slice(PAD + CH * j, PAD + CH * (j + 1))
             out = slice(CH * j, CH * (j + 1))
             col = jnp.where(lane == 0, pltpu.roll(tbuf[out], NCL - 8, 1), 0.0)
-            v[NPL, out] = jnp.where(up_z, pln[e, 1, out] - q_all[e, 0, NPL, rows] - col, 0.0)
-        v[NPL, 0:1] = v[NPL, 0:1] - jnp.where(jnp.logical_and(up_z, low_x), rcv[e, 4, 0:1], 0.0)
+            beyond = pln[e, 1, out] - q_all[e, 0, NPL, rows] - col
+            if j == 0:
+                beyond = beyond - jnp.where(jnp.logical_and(row == 0, low_x), rcv[e, 4, 0:1], 0.0)
+            v[NPL, out] = jnp.where(up_z, beyond, 0.0)
 
     def slopes(v, k, j):
         out = slice(CH * j, CH * (j + 1))
@@ -243,13 +247,12 @@
     send_last_plane(pm)
     send_first_plane(pm)
     send_tiles(pm)
-    send_last_plane(ps)
     loads[2].wait()
-    parts(ps, 0, True)
-    send_first_plane(ps)
-    for k in range(1, NPL):
+    for k in range(NPL):
         parts(ps, k, True)
     pack_tiles(ps)
+    send_first_plane(ps)
+    send_last_plane(ps)
     send_tiles(ps)
     loads[3].wait()
     loads[4].wait()
@@ -351,6 +354,7 @@
 
 def finish(hc, wg, u, dm, tcol, rrow, edge, dual_h, wg_h, dg_h, v, dual, dg, sem):
     lane = lax.broadcasted_iota(jnp.int32, (CH, NCL), 1)
+    row = lax.broadcasted_iota(jnp.int32, (CH, NCL), 0)
     copies = [pltpu.make_async_copy(wg, wg_h, sem.at[0])]
     copies[0].start()
     v[NPL, 0:NRW] = edge[1]
@@ -360,8 +364,9 @@
             total = u[k, out] - jnp.where(lane == 0, pltpu.roll(tcol[out], NCL - 2 * k - 1, 1), 0.0)
             if k == 0:
                 total = total - edge[0, out]
+            if j == 0:
+                total = total - jnp.where(row == 0, rrow[2 * k + 1 : 2 * k + 2], 0.0)
             v[k, out] = total
-        v[k, 0:1] = v[k, 0:1] - rrow[2 * k + 1 : 2 * k + 2]
         v[k, NRW : NRW + 1] = rrow[2 * k : 2 * k + 1]
         for j in range(NRW // CH):
             out = slice(CH * j, CH * (j + 1))

time: 21.8 us -> 21.7 us (level)
  no operation moved by 1% of the time
where the time goes in v6:
time: 21.7 us; the launch traced here: 21.6 us
  Pallas kernels  21 us (97%)
  between operations  0.64 us (3%)
    pallas_call x1, Pallas kernels, shards(): pl.pallas_call(functools.partial(kernel, sizes), out_shape=[jax.ShapeDtyp...  19.8 us
    pallas_call x1, Pallas kernels, shards(): pl.pallas_call(finish, out_shape=shapes, in_specs=[whole] * len(between),...  1.2 us

profile of v6, /device:TPU:103, one launch (start us, length us, event | category | flops | bytes accessed | tf_op | source)
XLA Modules:
  0.0 21.6 jit_solution(642217941850662250)
XLA Ops:
  0.6 19.8 %shard_map.76 = (f32[3,4,128,128]{3,2,1,0:T(8,128)S(1)}, f32[4,128,128]{2,1,0:T(8,128)S(1)}, f32[4,128,128]{2,1,0:T(8,128)S(1)}, f32[4,128,128]{2,1,0:T(8,128)S(...) custom-call(f32[4,128,128]{2,1,0:T(8,128)} %data_h.1, f32[4,128,128]{2,1,0:T(8,128)} %weight_h.1, ...), custom_call_target="tpu_custom_call" | custom-call | tf_op jit(solution)/shard_map/pallas_call | solution.py:402
  20.4 1.2 %shard_map.77 = (f32[3,4,128,128]{3,2,1,0:T(8,128)}, f32[4,128,128]{2,1,0:T(8,128)}, f32[4,128,128]{2,1,0:T(8,128)}) custom-call(f32[3,4,128,128]{3,2,1,0:T(8,128)S(1)} %get-tuple-element.10.hc, f32[4,128,128]{2,1,0:T(8,128)S(1)} %get-tuple-element.11.wg, f32[4,128,128]{2,1,0:T(8,128)S(1)} %get-tuple-element.12.u, f32[4,128,128]{2,1,0:T(8,128)S(1)} %get-tuple-element.13.dm, ...), custom_call_target="tpu_custom_call" | custom-call | tf_op jit(solution)/shard_map/pallas_call | solution.py:437

commit v7 on v5

--- a/solution.py
+++ b/solution.py
@@ -226,10 +226,11 @@
         send_first_plane(nxt)
         send_last_plane(nxt)
         fix(e, v, 2)
-        for k in (1, 2):
-            plane(body, k)
-            parts(nxt, k)
+        plane(body, 2)
         parts(nxt, 3)
+        plane(body, 1)
+        parts(nxt, 2)
+        parts(nxt, 1)
         pack_tiles(nxt)
         send_tiles(nxt)
 

time: 21.8 us -> 21.8 us (level)
  no operation moved by 1% of the time
where the time goes in v7:
time: 21.8 us; the launch traced here: 21.7 us
  Pallas kernels  21 us (96%)
  between operations  0.64 us (3%)
    pallas_call x1, Pallas kernels, shards(): pl.pallas_call(functools.partial(kernel, sizes), out_shape=[jax.ShapeDtyp...  19.8 us
    pallas_call x1, Pallas kernels, shards(): pl.pallas_call(finish, out_shape=shapes, in_specs=[whole] * len(between),...  1.22 us

profile of v7, /device:TPU:103, one launch (start us, length us, event | category | flops | bytes accessed | tf_op | source)
XLA Modules:
  0.0 21.7 jit_solution(8814224740147815288)
XLA Ops:
  0.6 19.8 %shard_map.76 = (f32[3,4,128,128]{3,2,1,0:T(8,128)S(1)}, f32[4,128,128]{2,1,0:T(8,128)S(1)}, f32[4,128,128]{2,1,0:T(8,128)S(1)}, f32[4,128,128]{2,1,0:T(8,128)S(...) custom-call(f32[4,128,128]{2,1,0:T(8,128)} %data_h.1, f32[4,128,128]{2,1,0:T(8,128)} %weight_h.1, ...), custom_call_target="tpu_custom_call" | custom-call | tf_op jit(solution)/shard_map/pallas_call | solution.py:398
  20.5 1.2 %shard_map.77 = (f32[3,4,128,128]{3,2,1,0:T(8,128)}, f32[4,128,128]{2,1,0:T(8,128)}, f32[4,128,128]{2,1,0:T(8,128)}) custom-call(f32[3,4,128,128]{3,2,1,0:T(8,128)S(1)} %get-tuple-element.10.hc, f32[4,128,128]{2,1,0:T(8,128)S(1)} %get-tuple-element.11.wg, f32[4,128,128]{2,1,0:T(8,128)S(1)} %get-tuple-element.12.u, f32[4,128,128]{2,1,0:T(8,128)S(1)} %get-tuple-element.13.dm, ...), custom_call_target="tpu_custom_call" | custom-call | tf_op jit(solution)/shard_map/pallas_call | solution.py:433
